TPU v7x, 32 devices: a whole 2x2x4 slice. The times are simulated.
32 devices in a mesh: space: 2 (over x), mrow: 4 (over y, core), mcol: 4 (over z).
Axes of the slice: x: 2, y: 2, z: 4, core: 2. Of those that a mesh axis runs over, the one named last changes fastest.
Arguments:
- deviation: bfloat16 [64, 48, 8192], P('space', None, ('mcol', 'mrow'))
- courant: float32 [2, 8192], P(None, ('mcol', 'mrow')), may hold values from -0.95 to 0.95
- collide: bfloat16 [8192, 8192], P('mrow', ('mcol', 'space'))
- hole_cells: int32 [768], P('space'), may hold values from -1 to 1535, as said below
- hole_wall: int32 [768], P('space'), may hold values from 0 to 3
- specular: int32 [4, 8192], replicated, may hold values from 0 to 8191, as said below
- specularity: float32 [4], replicated, may hold values from 0.2 to 0.8
Outputs:
- updated: bfloat16 [64, 48, 8192], P('space', None, ('mrow', 'mcol'))
Inputs may be any that keep to these rules, and one draw needn't show every extreme that they name: `hole_cells`: within one tile the used slots come first and name distinct cells; every tile has at least 96 used slots, some tile has all 384 slots used and some tile has an empty slot. Each row specular[w] is a permutation of the modes; for an outgoing mode i of aligned block e = i // 512, its incoming mode j lies, within j's own aligned block of 512 modes, in the sub-block of 32 modes numbered e, that is (j % 512) // 32 == e.
All inputs are finite; a program needn't handle non-finite values.
Results may differ from a plain program's by a relative error of at most 0.005.
Values may be sent and summed in bfloat16 or wider, within the bound.
No kernel may reach another device: no remote copies, remote signals or barrier semaphores. Data moves between devices by JAX's collectives and lax.ppermute only.
A program may use at most 128 MiB of HBM per device.

v0:
```python
import jax
import jax.numpy as jnp
from jax import lax
from jax.sharding import PartitionSpec as P


def extended(x, sides, width):
    for axis, dim in sides:
        size, length = (lax.axis_size(axis), x.shape[dim])
        up = [(i, (i + 1) % size) for i in range(size - 1)]
        down = [(j, i) for i, j in up]
        last = lax.slice_in_dim(x, length - width, length, axis=dim)
        first = lax.slice_in_dim(x, 0, width, axis=dim)
        before = lax.ppermute(last, axis, up)
        after = lax.ppermute(first, axis, down)
        x = jnp.concatenate([before, x, after], axis=dim)
    return x


def upwind(padded, courant):
    field = padded.astype(jnp.float32)
    reach_x = jnp.abs(courant[0])
    reach_y = jnp.abs(courant[1])
    center = field[1:-1]
    upwind_x = jnp.where(courant[0] > 0, field[:-2], field[2:])
    upwind_y = jnp.where(courant[1] > 0, jnp.roll(center, 1, axis=1), jnp.roll(center, -1, axis=1))
    upwind_xy = jnp.where(
        courant[1] > 0, jnp.roll(upwind_x, 1, axis=1), jnp.roll(upwind_x, -1, axis=1)
    )
    result = (1.0 - reach_x) * (1.0 - reach_y) * center + reach_x * (1.0 - reach_y) * upwind_x
    result = result + (1.0 - reach_x) * reach_y * upwind_y + reach_x * reach_y * upwind_xy
    return result.astype(jnp.bfloat16)


def mirror_values(source_rows, wall_tables, one_hot):
    flipped = source_rows.T
    picked = flipped[wall_tables].astype(jnp.float32)
    weights = one_hot.T.astype(jnp.float32)
    chosen = jnp.sum(weights[:, None, :] * picked, axis=0)
    return chosen.T


def on_device(deviation, courant, collide, hole_cells, hole_wall, specular, specularity):
    padded = extended(deviation, (("space", 0),), 1)
    read = upwind(padded, courant)
    width_x, width_y, block_len = read.shape
    cell_count = width_x * width_y
    row_groups = lax.axis_size("mrow")
    col_groups = lax.axis_size("mcol")
    is_live = hole_cells >= 0
    safe_ids = jnp.where(is_live, hole_cells, 0)
    target_ids = jnp.where(is_live, hole_cells, cell_count)
    wall_count = specular.shape[0]
    one_hot = hole_wall[:, None] == jnp.arange(wall_count, dtype=jnp.int32)[None, :]
    share = jnp.dot(one_hot.astype(jnp.float32), specularity, precision=lax.Precision.HIGHEST)
    flat_cells = read.reshape(cell_count, block_len)
    start = (lax.axis_index("mcol") * row_groups + lax.axis_index("mrow")) * block_len
    own_table = lax.dynamic_slice_in_dim(specular, start, block_len, 1)
    rim_local = flat_cells[safe_ids]
    slot_count = rim_local.shape[0]
    piece = block_len // (row_groups * col_groups)
    totals = lax.psum(jnp.sum(rim_local.astype(jnp.float32), axis=1), ("mrow", "mcol"))
    diffuse = totals / specular.shape[1]
    ordered = (
        rim_local.reshape(slot_count, col_groups, row_groups, piece)
        .transpose(0, 2, 1, 3)
        .reshape(slot_count, block_len)
    )
    arrived = lax.all_to_all(ordered, ("mrow", "mcol"), split_axis=1, concat_axis=1, tiled=True)
    block_ids = own_table // block_len
    positions = (
        block_ids % row_groups * col_groups + block_ids // row_groups
    ) * piece + own_table % piece
    mirrored = mirror_values(arrived, positions, one_hot)
    emitted = (share[:, None] * mirrored + (1.0 - share)[:, None] * diffuse[:, None]).astype(
        jnp.bfloat16
    )
    flat_cells = flat_cells.at[target_ids].set(emitted, mode="drop")
    columns = lax.all_gather(
        flat_cells.reshape(width_x, width_y, block_len), "mrow", axis=2, tiled=True
    )
    column_flat = columns.reshape(cell_count, columns.shape[2])
    partial_sums = lax.dot_general(
        column_flat,
        lax.all_gather(collide, "space", axis=1, tiled=True),
        (((1,), (1,)), ((), ())),
        preferred_element_type=jnp.float32,
    )
    summed = lax.psum_scatter(partial_sums, "mcol", scatter_dimension=1, tiled=True)
    return summed.astype(jnp.bfloat16).reshape(width_x, width_y, summed.shape[1])


def solution(mesh):
    in_specs = (
        P("space", None, ("mcol", "mrow")),
        P(None, ("mcol", "mrow")),
        P("mrow", ("mcol", "space")),
        P("space"),
        P("space"),
        P(),
        P(),
    )
    out_specs = P("space", None, ("mrow", "mcol"))
    return jax.shard_map(
        on_device, mesh=mesh, in_specs=in_specs, out_specs=out_specs, check_vma=False
    )
```

profile of v0, /device:TPU:20, one launch (start us, length us, event | category | flops | bytes accessed | tf_op | source)
XLA Modules:
  0.0 403.9 jit_solution(486045715008266758)
XLA Ops:
  6.6 0.7 all-gather.5.cloned.1.call-update
  7.3 0.7 copy-done.2
  8.0 3.4 collective-permute-start
  11.4 1.3 collective-permute-start.1
  12.7 0.5 compare_reduce_fusion
  13.2 0.6 fusion.18
  13.8 3.5 collective-permute-done.1
  17.4 0.3 maximum_convert_fusion
  17.7 0.6 slice_select_fusion
  18.3 0.7 fusion.22
  19.1 6.0 %fusion.20 = (f32[32,47,512]{2,1,0:T(8,128)}, f32[32,47,512]{2,1,0:T(8,128)}, f32[32,47,512]{2,1,0:T(8,128)}, f32[32,47,512]{2,1,0:T(8,128)}) fusion(f32[34,48,512]{2,1,0:T(8,128)S(1)} %maximum_convert_fusion, f32[32,48,512]{2,1,0:T(8,128)S(1)} %slice_select_fusion), kind=kLoop, calls=%fused_computation.64 | loop fusion | bytes 24641536 | tf_op jit(solution)/shard_map/jit(_roll_static)/slice | solution.py:26
  25.1 7.2 %fusion.3 = bf16[32,48,512]{2,1,0:T(8,128)(2,1)S(1)} fusion(f32[34,48,512]{2,1,0:T(8,128)S(1)} %maximum_convert_fusion, f32[32,47,512]{2,1,0:T(8,128)} %get-tuple-element.8, f32[32,1,512]{2,1,0:T(1,128)S(1)} %get-tuple-element.14, f32[32,1,512]{2,1,0:T(1,128)S(1)} %get-tuple-element.13, f32[32,47,512]{2,1,0:T(8,128)} %get-tuple-element.7, ...), kind=kLoop, calls=%fused_computation.8 | loop fusion | flops 11796480 | bytes 23602176 | tf_op jit(solution)/shard_map/convert_element_type | solution.py:32
  32.3 2.1 gather_fusion
  34.4 0.2 copy.10
  34.6 0.8 copy.11
  35.4 6.1 %all-to-all-start = ((bf16[384,16,32]{0,2,1:T(8,128)(2,1)}), bf16[384,16,32]{0,2,1:T(8,128)(2,1)S(1)}, u32[]{:S(2)}, u32[]{:S(2)}) async-start(bf16[384,16,32]{0,2,1:T(8,128)(2,1)} %bitcast.6), calls=%async_computation | async-start | bytes 786432 | tf_op jit(solution)/shard_map/all_to_all | solution.py:69
  41.5 0.7 fusion.17
  42.3 0.3 convolution_reduce_fusion
  42.8 31.5 %psum.7 = f32[384]{0:T(512)S(1)} all-reduce(f32[384]{0:T(512)S(1)} %convert_reduce_fusion), channel_id=1, replica_groups=mesh['space'=2,'mrow'=4,'mcol'=4] {'mrow','mcol'}, use_global_device_ids=true, to_apply=%region_2.3 | all-reduce | flops 384 | bytes 3072 | tf_op jit(solution)/shard_map/psum | solution.py:62
  74.3 0.6 multiply_multiply_fusion
  74.9 7.5 %gather_fusion.1 = bf16[2048,384]{1,0:T(8,128)(2,1)S(1)} fusion(bf16[512,384]{1,0:T(8,128)(2,1)S(1)} %bitcast.25, s32[2048]{0:T(1024)S(1)} %broadcast_clamp_fusion), kind=kCustom, calls=%fused_computation.1 | custom fusion | bytes 3153920 | tf_op jit(solution)/shard_map/gather | solution.py:37
  82.3 1.1 fusion.6
  83.4 0.8 fusion.7
  84.2 0.2 copy.12
  84.4 2.8 scatter_fusion
  87.2 1.1 copy-done.1
  88.4 0.2 reduce-scatter.2.cloned.1.call-start
  88.6 25.4 %all-gather.5.cloned.1.call-done = bf16[2048,2048]{1,0:T(8,128)(2,1)} async-done(((bf16[2048,1024]{1,0:T(8,128)(2,1)}), bf16[2048,2048]{1,0:T(8,128)(2,1)}) %all-gather.5.cloned.1.call-update) | async-done | bytes 8388624 | tf_op jit(solution)/shard_map/all_gather | solution.py:85
  114.0 47.1 %all-gather.3.cloned.1.call-done = bf16[32,48,2048]{2,1,0:T(8,128)(2,1)} async-done(((bf16[32,48,512]{2,1,0:T(8,128)(2,1)}), bf16[32,48,2048]{2,1,0:T(8,128)(2,1)}) %all-gather.3.cloned.1.call-update) | async-done | bytes 6291472 | tf_op jit(solution)/shard_map/all_gather | solution.py:79
  161.1 19.1 %fusion.24 = f32[1536,2048]{1,0:T(8,128)} fusion(bf16[1536,2048]{1,0:T(8,128)(2,1)} %bitcast.34, bf16[2048,2048]{1,0:T(8,128)(2,1)} %all-gather.5.cloned.1.call-done), kind=kOutput, calls=%fused_computation.68 | convolution fusion | flops 12884901888 | bytes 27262976 | tf_op jit(solution)/shard_map/dot_general | solution.py:83
  180.1 214.0 %reduce-scatter.2.cloned.1.call-done = f32[1536,512]{1,0:T(8,128)} async-done(((f32[1536,2048]{1,0:T(8,128)}), f32[1536,512]{1,0:T(8,128)}) %reduce-scatter.2.cloned.1.call-update) | async-done | bytes 3145744 | tf_op jit(solution)/shard_map/reduce_scatter | solution.py:89
  394.1 3.2 convert_element_type.36
  (35 shorter events, 0.4 us)
Async XLA Ops:
  6.5 35.7 %copy-start = (f32[4]{0:T(128)S(1)}, f32[4]{0:T(128)}, u32[]{:S(2)}) copy-start(f32[4]{0:T(128)} %param.13) | copy-start | bytes 52
  6.5 1.4 copy-start.2
  6.5 6.1 %copy-start.3 = (f32[2,512]{1,0:T(2,128)S(1)}, f32[2,512]{1,0:T(2,128)}, u32[]{:S(2)}) copy-start(f32[2,512]{1,0:T(2,128)} %param.8) | copy-start | bytes 12292
  6.5 6.6 %copy-start.8 = (s32[384]{0:T(512)S(1)}, s32[384]{0:T(512)}, u32[]{:S(2)}) copy-start(s32[384]{0:T(512)} %param.10) | copy-start | bytes 4612
  6.5 6.7 %copy-start.9 = (s32[384]{0:T(512)S(1)}, s32[384]{0:T(512)}, u32[]{:S(2)}) copy-start(s32[384]{0:T(512)} %param.11) | copy-start | bytes 4612
  6.6 107.4 %all-gather.5.cloned.1.call-start = ((), (), s32[]{:S(2)}) async-start(), calls=%async_computation.3 | async-start | bytes 12582912 | tf_op jit(solution)/shard_map/all_gather | solution.py:85
  8.0 5.9 %collective-permute-start = (bf16[1,48,512]{2,1,0:T(8,128)(2,1)S(1)}, bf16[1,48,512]{2,1,0:T(8,128)(2,1)S(1)}, u32[]{:S(2)}, u32[]{:S(2)}) collective-permute-start(bf16[1,48,512]{2,1,0:T(8,128)(2,1)S(1)} %get-tuple-element.15), channel_id=1, source_target_pairs={{0,16},{1,17},{2,18},{3,19},{4,20},{5,21},{6,22},{7,23},{8,24},{9,... | collective-permute-start | bytes 147464 | tf_op jit(solution)/shard_map/ppermute | solution.py:14
  11.4 6.0 %collective-permute-start.1 = (bf16[1,48,512]{2,1,0:T(8,128)(2,1)S(1)}, bf16[1,48,512]{2,1,0:T(8,128)(2,1)S(1)}, u32[]{:S(2)}, u32[]{:S(2)}) collective-permute-start(bf16[1,48,512]{2,1,0:T(8,128)(2,1)S(1)} %get-tuple-element.16), channel_id=1, source_target_pairs={{16,0},{17,1},{18,2},{19,3},{20,4},{21,5},{22,6},{23,7},{24,8},{25... | collective-permute-start | bytes 147464 | tf_op jit(solution)/shard_map/ppermute | solution.py:15
  13.2 4.5 %copy-start.5 = (pred[512]{0:T(512)(128)(4,1)}, pred[512]{0:T(512)(128)(4,1)S(1)}, u32[]{:S(2)}) copy-start(pred[512]{0:T(512)(128)(4,1)S(1)} %get-tuple-element.6) | copy-start | bytes 1540
  19.1 6.0 %copy-start.6 = (pred[512]{0:T(512)(128)(4,1)S(1)}, pred[512]{0:T(512)(128)(4,1)}, u32[]{:S(2)}) copy-start(pred[512]{0:T(512)(128)(4,1)} %copy-done.5) | copy-start | bytes 1540
  19.1 6.0 %copy-start.7 = (pred[512]{0:T(512)(128)(4,1)S(1)}, pred[512]{0:T(512)(128)(4,1)}, u32[]{:S(2)}) copy-start(pred[512]{0:T(512)(128)(4,1)} %get-tuple-element.5) | copy-start | bytes 1540
  32.3 10.0 %copy-start.10 = (s32[384]{0:T(512)S(1)}, s32[384]{0:T(512)}, u32[]{:S(2)}) copy-start(s32[384]{0:T(512)} %param.11) | copy-start | bytes 4612
  35.4 39.5 %all-to-all-start = ((bf16[384,16,32]{0,2,1:T(8,128)(2,1)}), bf16[384,16,32]{0,2,1:T(8,128)(2,1)S(1)}, u32[]{:S(2)}, u32[]{:S(2)}) async-start(bf16[384,16,32]{0,2,1:T(8,128)(2,1)} %bitcast.6), calls=%async_computation | async-start | bytes 786432 | tf_op jit(solution)/shard_map/all_to_all | solution.py:69
  41.5 119.6 %all-gather.3.cloned.1.call-start = ((), (), s32[]{:S(2)}) async-start(), calls=%async_computation.2 | async-start | bytes 7864320 | tf_op jit(solution)/shard_map/all_gather | solution.py:79
  42.6 32.3 %copy-start.4 = (f32[384]{0:T(512)}, f32[384]{0:T(512)S(1)}, u32[]{:S(2)}) copy-start(f32[384]{0:T(512)S(1)} %convolution_reduce_fusion) | copy-start | bytes 4612
  87.2 1.1 copy-start.1
  88.4 305.7 %reduce-scatter.2.cloned.1.call-start = ((), (), s32[]{:S(2)}) async-start(), calls=%async_computation.4 | async-start | bytes 15728640 | tf_op jit(solution)/shard_map/reduce_scatter | solution.py:89
Sparse Core Ops, SparseCore 0:
  8.9 105.0 all-gather.4
  115.6 45.4 all-gather.2
  180.3 213.8 reduce-scatter.1
where the time goes:
time: 405 us; the launch traced here: 404 us
  waiting for transfers between devices  291 us (72%)
  blocking collectives  31.5 us (8%)
  local copies, waits for them, and re-layouts  22.1 us (5%)
  matrix products  19.4 us (5%)
  other arithmetic  15.8 us (4%)
  between operations  13.3 us (3%)
  starting transfers between devices  11.1 us (3%)
    reduce_scatter x1, waiting for transfers between devices, on_device(): lax.psum_scatter(partial_sums, 'mcol', scatter_dimension=1, tiled=True)  214 us
    all_gather x1, waiting for transfers between devices, on_device(): lax.all_gather(flat_cells.reshape(width_x, width_y, block_len), 'mrow', a...  47.1 us
    psum x1, blocking collectives, on_device(): lax.psum(jnp.sum(rim_local.astype(jnp.float32), axis=1), ('mrow', 'mcol'))  31.5 us
    all_gather x1, waiting for transfers between devices, on_device(): lax.all_gather(collide, 'space', axis=1, tiled=True)  25.4 us
    dot_general x1, matrix products, on_device(): lax.dot_general(column_flat, lax.all_gather(collide, 'space', axis=1, til...  19.1 us
  transfers between devices with their start and end apart: 6, of which 4 were waited for; matrix products, arithmetic and copies ran while one was open for 8% of the time, Pallas kernels for 0%

commit v1 on v0

v1 whole, which is shorter than its diff:
```python
import functools
import jax
import jax.numpy as jnp
import numpy as np
from jax import lax
from jax.experimental import pallas as pl
from jax.experimental.pallas import tpu as pltpu
from jax.sharding import PartitionSpec as P

VMEM = pltpu.VMEM
SMEM = pltpu.SMEM
ANY = pl.ANY
NT = (((1,), (1,)), ((), ()))
LIMIT = 48 * 1024 * 1024
CELL_CHUNKS = 3
TAIL = 16


def line_steps(size):
    order = []
    for c in range(size):
        row = []
        for t in range(1, size):
            if c <= t - 1:
                row.append(c + size - t)
            if c >= size - t:
                row.append(c - size + t)
        row.append(c)
        order.append(row)
    return np.array(order, np.int32)


def slot_of(c, t, size):
    place = 0
    for u in range(1, t):
        place = place + jnp.where(c <= u - 1, 1, 0) + jnp.where(c >= size - u, 1, 0)
    return place


def slots_at(t, size):
    found = set()
    for c in range(size):
        place = 0
        for u in range(1, size):
            for hit in (c <= u - 1, c >= size - u):
                if hit:
                    if u == t:
                        found.add(place)
                    place += 1
        if t == size:
            found.add(size - 1)
    return sorted(found)


def read_kernel(rows_of, cols_of, dev, before, after, courant, select, read, payload):
    width_x, width_y, modes = dev.shape
    speed = courant[...]
    reach = jnp.abs(speed)
    ahead = speed > 0
    a = jnp.broadcast_to(reach[0:1], (width_y, modes))
    b = jnp.broadcast_to(reach[1:2], (width_y, modes))
    ahead_x = jnp.broadcast_to(ahead[0:1], (width_y, modes))
    ahead_y = jnp.broadcast_to(ahead[1:2], (width_y, modes))

    def one(x, low, high):
        center = dev[x].astype(jnp.float32)
        ux = jnp.where(ahead_x, low.astype(jnp.float32), high.astype(jnp.float32))
        along = (1.0 - a) * center + a * ux
        shifted = jnp.where(ahead_y, pltpu.roll(along, 1, 0), pltpu.roll(along, width_y - 1, 0))
        read[pl.ds(pl.multiple_of(x * width_y, 16), width_y), :] = (
            (1.0 - b) * along + b * shifted
        ).astype(read.dtype)

    one(0, before[0], dev[1])

    def body(x, carry):
        one(x, dev[x - 1], dev[x + 1])
        return carry

    lax.fori_loop(1, width_x - 1, body, 0)
    one(width_x - 1, dev[width_x - 2], after[0])

    rim = lax.dot_general(
        select[...], read[...], (((1,), (0,)), ((), ())), preferred_element_type=jnp.float32
    )
    flipped = rim.T
    total = jnp.sum(flipped, axis=0, keepdims=True)
    high = total.astype(jnp.bfloat16).astype(jnp.float32)
    middle = (total - high).astype(jnp.bfloat16).astype(jnp.float32)
    low = total - high - middle
    place = lax.broadcasted_iota(jnp.int32, (TAIL, total.shape[1]), 0)
    tail = jnp.where(place == 0, high, jnp.where(place == 1, middle, jnp.where(place == 2, low, 0.0)))
    tail = tail.astype(jnp.bfloat16)
    piece = modes // (rows_of * cols_of)
    packed = flipped.astype(jnp.bfloat16)
    for r in range(rows_of):
        for c in range(cols_of):
            block = c * rows_of + r
            payload[r * cols_of + c, 0:piece, :] = packed[block * piece : (block + 1) * piece]
            payload[r * cols_of + c, piece : piece + TAIL, :] = tail


def rim_kernel(mode_count, specularity, read, arrived, mirror, place, on_rim, wall, *outs):
    groups, height, slots = arrived.shape
    piece = height - TAIL
    values = arrived[:, 0:piece, :].reshape(groups * piece, slots)
    sums = arrived[:, piece:height, :].reshape(groups * TAIL, slots).astype(jnp.float32)
    diffuse = jnp.sum(sums, axis=0, keepdims=True) / mode_count
    walls = wall[...]
    share = jnp.zeros(walls.shape, jnp.float32)
    mirrored = jnp.zeros((groups * piece, slots), jnp.float32)
    for w in range(mirror.shape[0]):
        share = jnp.where(walls == w, specularity[w], share)
        picked = lax.dot_general(
            mirror[w], values, (((1,), (0,)), ((), ())), preferred_element_type=jnp.float32
        )
        mirrored = jnp.where(walls == w, picked, mirrored)
    emitted = (share * mirrored + (1.0 - share) * diffuse).astype(jnp.bfloat16)
    step = outs[0].shape[0]
    for n, out in enumerate(outs):
        rows = slice(n * step, (n + 1) * step)
        spread = lax.dot_general(place[rows, :], emitted, NT, preferred_element_type=jnp.float32)
        out[...] = jnp.where(on_rim[rows, :] > 0, spread, read[rows, :].astype(jnp.float32)).astype(
            out.dtype
        )


def hop_kernel(t, size, wide, slots, has_recv, *refs):
    refs = list(refs)
    where = refs.pop(0)
    blocks = [refs.pop(0) for _ in range(4)]
    own = refs.pop(0)
    others = {j: refs.pop(0) for j in slots}
    final = t == size
    recv = [refs.pop(0), refs.pop(0)] if has_recv else None
    outs = [refs.pop(0)] if final else [refs.pop(0), refs.pop(0)]
    buffer, sem = refs
    s, r, c = where[0], where[1], where[2]
    rows = buffer.shape[1]
    width = blocks[0].shape[1]
    if final:
        jobs = [(c, None, size - 1)]
    else:
        first = slot_of(c, t, size)
        goes_right = c <= t - 1
        jobs = [
            (c + size - t, goes_right, first),
            (c - size + t, c >= size - t, first + jnp.where(goes_right, 1, 0)),
        ]

    def fetch(n, d, place):
        for b in range(4):
            source = lax.bitwise_xor(r, b)
            target = buffer.at[n, :, b * width : (b + 1) * width]
            if wide:
                column = pl.multiple_of(source * width, width)
                pltpu.make_async_copy(
                    own.at[pl.ds(pl.multiple_of(d * rows, rows), rows), pl.ds(column, width)],
                    target,
                    sem.at[n],
                ).start()
                continue
            column = pl.multiple_of(lax.bitwise_and(source, 1) * width, width)
            is_own = lax.shift_right_logical(source, 1) == s

            @pl.when(is_own)
            def _():
                pltpu.make_async_copy(
                    own.at[pl.ds(pl.multiple_of(d * rows, rows), rows), pl.ds(column, width)],
                    target,
                    sem.at[n],
                ).start()

            for j, other in others.items():

                @pl.when(jnp.logical_and(jnp.logical_not(is_own), place == j))
                def _(other=other):
                    pltpu.make_async_copy(other.at[:, pl.ds(column, width)], target, sem.at[n]).start()

    def multiply(n, out):
        pltpu.make_async_copy(buffer.at[n], buffer.at[n], sem.at[n]).wait()
        total = None
        for b in range(4):
            part = lax.dot_general(
                blocks[b][...],
                buffer[n, :, b * width : (b + 1) * width],
                NT,
                preferred_element_type=jnp.float32,
            )
            total = part if total is None else total + part
        if final:
            total = total + recv[0][...].astype(jnp.float32) + recv[1][...].astype(jnp.float32)
        elif has_recv:
            total = total + recv[n][...].astype(jnp.float32)
        out[...] = total.astype(out.dtype)

    for n, (d, valid, place) in enumerate(jobs):
        if valid is None:
            fetch(n, d, place)
        else:
            pl.when(valid)(functools.partial(fetch, n, d, place))
    for n, (d, valid, place) in enumerate(jobs):
        if valid is None:
            multiply(n, outs[n])
        else:
            pl.when(valid)(functools.partial(multiply, n, outs[n]))


def hop(t, size, wide, where, blocks, own, others, recv):
    slots = () if wide else tuple(slots_at(t, size))
    rows = own.shape[0] // size
    cells, width = blocks[0].shape
    count = 1 if t == size else 2
    spec = pl.BlockSpec(memory_space=VMEM)
    any_spec = pl.BlockSpec(memory_space=ANY)
    operands = [where, *blocks, own, *[others[j] for j in slots], *(recv or [])]
    in_specs = [pl.BlockSpec(memory_space=SMEM)] + [spec] * 4 + [any_spec] * (1 + len(slots))
    in_specs += [spec] * len(recv or [])
    return pl.pallas_call(
        functools.partial(hop_kernel, t, size, wide, slots, recv is not None),
        out_shape=[jax.ShapeDtypeStruct((cells, rows), jnp.bfloat16)] * count,
        in_specs=in_specs,
        out_specs=[spec] * count,
        scratch_shapes=[
            pltpu.VMEM((count, rows, 4 * width), jnp.bfloat16),
            pltpu.SemaphoreType.DMA((count,)),
        ],
        compiler_params=pltpu.CompilerParams(vmem_limit_bytes=LIMIT),
        cost_estimate=pl.CostEstimate(
            flops=2 * cells * rows * width * 4, bytes_accessed=8 * cells * width * 2, transcendentals=0
        ),
    )(*operands)


def on_device(deviation, courant, collide, hole_cells, hole_wall, specular, specularity):
    n_space, n_row, n_col = (lax.axis_size(name) for name in ("space", "mrow", "mcol"))
    s, r, c = (lax.axis_index(name) for name in ("space", "mrow", "mcol"))
    width_x, width_y, block_len = deviation.shape
    cell_count = width_x * width_y
    slot_count = hole_cells.shape[0]
    wall_count, mode_count = specular.shape
    piece = block_len // (n_row * n_col)
    groups = n_row * n_col
    vmem = pl.BlockSpec(memory_space=VMEM)
    params = pltpu.CompilerParams(vmem_limit_bytes=LIMIT)
    where = jnp.stack([s, r, c]).astype(jnp.int32)

    up = [(i, i + 1) for i in range(n_space - 1)]
    down = [(j, i) for i, j in up]
    before = lax.ppermute(deviation[-1:], "space", up)
    after = lax.ppermute(deviation[:1], "space", down)

    cells = jnp.arange(cell_count, dtype=jnp.int32)
    select = (hole_cells[:, None] == cells[None, :]).astype(jnp.bfloat16)
    place = (cells[:, None] == hole_cells[None, :]).astype(jnp.bfloat16)
    on_rim = jnp.max(place.astype(jnp.float32), axis=1, keepdims=True)
    own_table = lax.dynamic_slice_in_dim(specular, (c * n_row + r) * block_len, block_len, 1)
    source = own_table // block_len
    positions = (source % n_row * n_col + source // n_row) * piece + own_table % piece
    mirror = (
        positions[:, :, None] == jnp.arange(block_len, dtype=jnp.int32)[None, None, :]
    ).astype(jnp.bfloat16)

    wide = n_space != 2
    rows = collide.shape[0] // n_col
    others = []
    if wide:
        own = lax.all_gather(collide, "space", axis=1, tiled=True)
    else:
        own = collide
        order = jnp.asarray(line_steps(n_col))
        token = (before, after)
        for j in range(n_col):
            part = lax.dynamic_slice_in_dim(collide, order[c, j] * rows, rows, 0)
            part, token = lax.optimization_barrier((part, token))
            got = lax.ppermute(part, "space", [(0, 1), (1, 0)])
            others.append(got)
            token = got
            if j == 0:
                before, after = before, after

    read, payload = pl.pallas_call(
        functools.partial(read_kernel, n_row, n_col),
        out_shape=[
            jax.ShapeDtypeStruct((cell_count, block_len), jnp.bfloat16),
            jax.ShapeDtypeStruct((groups, piece + TAIL, slot_count), jnp.bfloat16),
        ],
        in_specs=[vmem] * 5,
        out_specs=[vmem] * 2,
        compiler_params=params,
    )(deviation, before, after, courant, select)
    arrived = lax.all_to_all(payload, ("mrow", "mcol"), split_axis=0, concat_axis=0, tiled=True)
    step = cell_count // CELL_CHUNKS
    own_chunks = pl.pallas_call(
        functools.partial(rim_kernel, mode_count),
        out_shape=[jax.ShapeDtypeStruct((step, block_len), jnp.bfloat16)] * CELL_CHUNKS,
        in_specs=[pl.BlockSpec(memory_space=SMEM)] + [vmem] * 6,
        out_specs=[vmem] * CELL_CHUNKS,
        compiler_params=params,
    )(specularity, read, arrived, mirror, place, on_rim, hole_wall[None, :])

    flip = [[(i, i ^ bit) for i in range(n_row)] for bit in (1, 2)]
    chunks = []
    for mine in own_chunks:
        far = lax.ppermute(mine, "mrow", flip[1])
        near = lax.ppermute(mine, "mrow", flip[0])
        both = lax.ppermute(far, "mrow", flip[0])
        chunks.append([mine, near, far, both])

    right = [(i, i + 1) for i in range(n_col - 1)]
    left = [(j, i) for i, j in right]
    state = [None] * CELL_CHUNKS
    for t in range(1, n_col):
        for n in range(CELL_CHUNKS):
            to_right, to_left = hop(t, n_col, wide, where, chunks[n], own, others, state[n])
            state[n] = [
                lax.ppermute(to_right, "mcol", right[:t]),
                lax.ppermute(to_left, "mcol", left[n_col - 1 - t :]),
            ]
    outs = [
        hop(n_col, n_col, wide, where, chunks[n], own, others, state[n])[0] for n in range(CELL_CHUNKS)
    ]
    return jnp.concatenate(outs, axis=0).reshape(width_x, width_y, rows)


def solution(mesh):
    in_specs = (
        P("space", None, ("mcol", "mrow")),
        P(None, ("mcol", "mrow")),
        P("mrow", ("mcol", "space")),
        P("space"),
        P("space"),
        P(),
        P(),
    )
    out_specs = P("space", None, ("mrow", "mcol"))
    return jax.shard_map(
        on_device, mesh=mesh, in_specs=in_specs, out_specs=out_specs, check_vma=False
    )
```

time: 405 us -> 204 us (0.50)
  waiting for transfers between devices: 291 us -> 67.2 us
  Pallas kernels: 0 us -> 49.8 us
  starting transfers between devices: 11.1 us -> 57.5 us
  blocking collectives: 31.5 us -> 0 us
  matrix products: 19.4 us -> 0 us
  between operations: 13.3 us -> 3.11 us
  other arithmetic: 15.8 us -> 6.44 us
    reduce_scatter x1 -> x0, waiting for transfers between devices: 214 us -> none  [on_device(): lax.psum_scatter(partial_sums, 'mcol', scatter_dimension=1, tiled=True)]
    all_gather x2 -> x0, waiting for transfers between devices: 72.4 us -> none  [the longest x1 47.1 us: on_device(): lax.all_gather(flat_cells.reshape(width_x, width_y, block_len), 'mrow', a...]
    ppermute x2 -> x33, waiting for transfers between devices: 3.5 us -> 64.9 us  [the longest x9 34.8 us: on_device(): lax.ppermute(to_left, 'mcol', left[n_col - 1 - t:])]
    pallas_call x0 -> x14, Pallas kernels: none -> 49.8 us  [the longest x12 42.3 us: hop(): pl.pallas_call(functools.partial(hop_kernel, t, size, wide, slots, recv i...]
    ppermute x2 -> x33, starting transfers between devices: 4.68 us -> 51.3 us  [the longest x9 21.1 us: on_device(): lax.ppermute(to_left, 'mcol', left[n_col - 1 - t:])]
    psum x1 -> x0, blocking collectives: 31.5 us -> none  [on_device(): lax.psum(jnp.sum(rim_local.astype(jnp.float32), axis=1), ('mrow', 'mcol'))]
    dot_general x2 -> x0, matrix products: 19.4 us -> none  [the longest x1 19.1 us: on_device(): lax.dot_general(column_flat, lax.all_gather(collide, 'space', axis=1, til...]
    gather x3 -> x0, local copies, waits for them, and re-layouts: 9.73 us -> none  [the longest x1 7.45 us: mirror_values(): picked = flipped[wall_tables].astype(jnp.float32)]
  transfers between devices with their start and end apart: 6 -> 34, of which waited for: 4 -> 13; matrix products, arithmetic and copies ran while one was open for 8% -> 6% of each run, Pallas kernels for 0% -> 21%
where the time goes in v1:
time: 204 us; the launch traced here: 202 us
  waiting for transfers between devices  67.2 us (33%)
  starting transfers between devices  57.5 us (28%)
  Pallas kernels  49.8 us (24%)
  local copies, waits for them, and re-layouts  18.4 us (9%)
  other arithmetic  6.44 us (3%)
  between operations  3.11 us (2%)
    pallas_call x12, Pallas kernels, hop(): pl.pallas_call(functools.partial(hop_kernel, t, size, wide, slots, recv i...  42.3 us
    ppermute x9, waiting for transfers between devices, on_device(): lax.ppermute(to_left, 'mcol', left[n_col - 1 - t:])  34.8 us
    ppermute x3, waiting for transfers between devices, on_device(): far = lax.ppermute(mine, 'mrow', flip[1])  22.3 us
    ppermute x9, starting transfers between devices, on_device(): lax.ppermute(to_left, 'mcol', left[n_col - 1 - t:])  21.1 us
    ppermute x9, starting transfers between devices, on_device(): lax.ppermute(to_right, 'mcol', right[:t])  12.6 us
    unnamed x38, local copies, waits for them, and re-layouts  11.5 us
    ppermute x4, starting transfers between devices, on_device(): got = lax.ppermute(part, 'space', [(0, 1), (1, 0)])  9 us
    ppermute x4, waiting for transfers between devices, on_device(): got = lax.ppermute(part, 'space', [(0, 1), (1, 0)])  7.73 us
  transfers between devices with their start and end apart: 34, of which 13 were waited for; matrix products, arithmetic and copies ran while one was open for 6% of the time, Pallas kernels for 21%

profile of v1, /device:TPU:20, one launch (start us, length us, event | category | flops | bytes accessed | tf_op | source)
XLA Modules:
  0.0 202.3 jit_solution(9917748366844711353)
XLA Ops:
  0.8 3.4 %collective-permute-start = (bf16[1,48,512]{2,1,0:T(8,128)(2,1)S(1)}, bf16[1,48,512]{2,1,0:T(8,128)(2,1)S(1)}, u32[]{:S(2)}, u32[]{:S(2)}) collective-permute-start(bf16[1,48,512]{2,1,0:T(8,128)(2,1)S(1)} %get-tuple-element.64), channel_id=1, source_target_pairs={{0,16},{1,17},{2,18},{3,19},{4,20},{5,21},{6,22},{7,23},{8,24},{9,... | collective-permute-start | bytes 147464 | tf_op jit(solution)/shard_map/ppermute | solution.py:250
  12.6 3.6 %shard_map.82 = (bf16[1536,512]{1,0:T(8,128)(2,1)S(1)}, bf16[16,48,384]{2,1,0:T(8,128)(2,1)}) custom-call(bf16[32,48,512]{2,1,0:T(8,128)(2,1)S(1)} %copy-done.9, bf16[1,48,512]{2,1,0:T(8,128)(2,1)S(1)} %collective-permute-done.before, bf16[1,48,512]{2,1,0:T(8,128)(2,1)S(1)} %collective-permute-done.1.after, f32[2,512]{1,0:T(2,128)S(1)} %copy-done.12, ...), custom_call_target="tpu_custom_call" | custom-call | tf_op jit(solution)/shard_map/pallas_call | solution.py:282
  17.4 6.1 %all-to-all-start = ((bf16[16,48,384]{2,1,0:T(8,128)(2,1)}), bf16[16,48,384]{2,1,0:T(8,128)(2,1)S(1)}, u32[]{:S(2)}, u32[]{:S(2)}) async-start(bf16[16,48,384]{2,1,0:T(8,128)(2,1)} %get-tuple-element.33), calls=%async_computation | async-start | bytes 1179648 | tf_op jit(solution)/shard_map/all_to_all | solution.py:292
  23.6 4.3 %constant_dynamic-slice_fusion = (bf16[512,1024]{1,0:T(8,128)(2,1)}, bf16[512,1024]{1,0:T(8,128)(2,1)}, bf16[512,1024]{1,0:T(8,128)(2,1)}, bf16[512,1024]{1,0:T(8,128)(2,1)}) fusion(bf16[2048,1024]{1,0:T(8,128)(2,1)} %refs_5_.23, s32[]{:T(128)S(6)} %select_n.49, s32[]{:T(128)S(6)} %select_n.48, s32[]{:T(128)S(6)} %select_n.47, s32[]{:T(128)S(6)} %select_n.46), kind=kLoop, calls=%fused_computation.29 | loop fusion | bytes 8388624 | tf_op jit(solution)/shard_map/dynamic_slice | solution.py:274
  27.8 2.6 %collective-permute-start.5 = (bf16[512,1024]{1,0:T(8,128)(2,1)}, bf16[512,1024]{1,0:T(8,128)(2,1)S(1)}, u32[]{:S(2)}, u32[]{:S(2)}) collective-permute-start(bf16[512,1024]{1,0:T(8,128)(2,1)} %get-tuple-element.35), channel_id=1, source_target_pairs={{0,16},{16,0},{1,17},{17,1},{2,18},{18,2},{3,19},{19,3},{4,20},{20... | collective-permute-start | bytes 3145736 | tf_op jit(solution)/shard_map/ppermute | solution.py:276
  34.9 2.2 %all-to-all-done.arrived = bf16[16,48,384]{2,1,0:T(8,128)(2,1)S(1)} async-done(((bf16[16,48,384]{2,1,0:T(8,128)(2,1)}), bf16[16,48,384]{2,1,0:T(8,128)(2,1)S(1)}, u32[]{:S(2)}, u32[]{:S(2)}) %all-to-all-start) | async-done | bytes 589856 | tf_op jit(solution)/shard_map/all_to_all | solution.py:292
  41.8 3.8 %shard_map.83 = (bf16[512,512]{1,0:T(8,128)(2,1)S(1)}, bf16[512,512]{1,0:T(8,128)(2,1)S(1)}, bf16[512,512]{1,0:T(8,128)(2,1)S(1)}) custom-call(f32[4]{0:T(128)S(1)} %copy-done.13, bf16[1536,512]{1,0:T(8,128)(2,1)S(1)} %copy-done.11, bf16[16,48,384]{2,1,0:T(8,128)(2,1)S(1)} %copy-done.8, bf16[4,512,512]{2,1,0:T(8,128)(2,1)} %fusion.mirror, ...), custom_call_target="tpu_custom_call" | custom-call | tf_op jit(solution)/shard_map/pallas_call | solution.py:294
  46.4 7.7 %collective-permute-done.5.refs_6_ = bf16[512,1024]{1,0:T(8,128)(2,1)S(1)} collective-permute-done((bf16[512,1024]{1,0:T(8,128)(2,1)}, bf16[512,1024]{1,0:T(8,128)(2,1)S(1)}, u32[]{:S(2)}, u32[]{:S(2)}) %collective-permute-start.5) | collective-permute-done | bytes 1048608 | tf_op jit(solution)/shard_map/ppermute | solution.py:276
  60.6 10.9 %collective-permute-done.16.refs_3_ = bf16[512,512]{1,0:T(8,128)(2,1)} collective-permute-done((bf16[512,512]{1,0:T(8,128)(2,1)S(1)}, bf16[512,512]{1,0:T(8,128)(2,1)}, u32[]{:S(2)}, u32[]{:S(2)}) %collective-permute-start.16) | collective-permute-done | bytes 524320 | tf_op jit(solution)/shard_map/ppermute | solution.py:305
  71.5 10.8 %collective-permute-done.3.refs_3_ = bf16[512,512]{1,0:T(8,128)(2,1)} collective-permute-done((bf16[512,512]{1,0:T(8,128)(2,1)S(1)}, bf16[512,512]{1,0:T(8,128)(2,1)}, u32[]{:S(2)}, u32[]{:S(2)}) %collective-permute-start.3) | collective-permute-done | bytes 524320 | tf_op jit(solution)/shard_map/ppermute | solution.py:305
  87.1 2.1 %collective-permute-start.7 = (bf16[512,1024]{1,0:T(8,128)(2,1)S(1)}, bf16[512,1024]{1,0:T(8,128)(2,1)S(1)}, u32[]{:S(2)}, u32[]{:S(2)}) collective-permute-start(bf16[512,1024]{1,0:T(8,128)(2,1)S(1)} %copy-done.16), channel_id=1, source_target_pairs={{0,16},{16,0},{1,17},{17,1},{2,18},{18,2},{3,19},{19,3},{4,20},{20... | collective-permute-start | bytes 3145736 | tf_op jit(solution)/shard_map/ppermute | solution.py:276
  95.8 12.6 %collective-permute-done.28.refs_9_ = bf16[512,512]{1,0:T(8,128)(2,1)S(1)} collective-permute-done((bf16[512,512]{1,0:T(8,128)(2,1)S(1)}, bf16[512,512]{1,0:T(8,128)(2,1)S(1)}, u32[]{:S(2)}, u32[]{:S(2)}) %collective-permute-start.28) | collective-permute-done | bytes 524320 | tf_op jit(solution)/shard_map/ppermute | solution.py:318
  109.7 3.9 %shard_map.93 = (bf16[512,512]{1,0:T(8,128)(2,1)S(1)}, bf16[512,512]{1,0:T(8,128)(2,1)S(1)}) custom-call(s32[3]{0:T(128)S(1)} %pad_add_fusion.refs_0_, bf16[512,512]{1,0:T(8,128)(2,1)S(1)} %copy-done.3, bf16[512,512]{1,0:T(8,128)(2,1)S(1)} %copy-done.5, bf16[512,512]{1,0:T(8,128)(2,1)} %collective-permute-done.25.refs_3_, ...), custom_call_target="tpu_custom_call" | custom-call | flops 1073741824 | bytes 4194304 | tf_op jit(solution)/shard_map/pallas_call | solution.py:219
  115.0 4.7 %collective-permute-done.19.refs_9_ = bf16[512,512]{1,0:T(8,128)(2,1)S(1)} collective-permute-done((bf16[512,512]{1,0:T(8,128)(2,1)S(1)}, bf16[512,512]{1,0:T(8,128)(2,1)S(1)}, u32[]{:S(2)}, u32[]{:S(2)}) %collective-permute-start.19) | collective-permute-done | bytes 524320 | tf_op jit(solution)/shard_map/ppermute | solution.py:318
  121.7 3.9 %shard_map.89 = (bf16[512,512]{1,0:T(8,128)(2,1)S(1)}, bf16[512,512]{1,0:T(8,128)(2,1)S(1)}) custom-call(s32[3]{0:T(128)S(1)} %pad_add_fusion.refs_0_, bf16[512,512]{1,0:T(8,128)(2,1)S(1)} %get-tuple-element.45.refs_1_, bf16[512,512]{1,0:T(8,128)(2,1)} %collective-permute-done.15.refs_2_, bf16[512,512]{1,0:T(8,128)(2,1)} %collective-permute-done.16.refs_3_, ...), custom_call_target="tpu_custom_call" | custom-call | flops 1073741824 | bytes 4194304 | tf_op jit(solution)/shard_map/pallas_call | solution.py:219
  127.0 5.7 %collective-permute-start.21 = (bf16[512,512]{1,0:T(8,128)(2,1)S(1)}, bf16[512,512]{1,0:T(8,128)(2,1)S(1)}, u32[]{:S(2)}, u32[]{:S(2)}) collective-permute-start(bf16[512,512]{1,0:T(8,128)(2,1)S(1)} %get-tuple-element.49), channel_id=1, source_target_pairs={{2,1},{3,2},{6,5},{7,6},{10,9},{11,10},{14,13},{15,14},{18,17},{19... | collective-permute-start | bytes 1572872 | tf_op jit(solution)/shard_map/ppermute | solution.py:318
  132.7 2.5 %collective-permute-start.8 = (bf16[512,1024]{1,0:T(8,128)(2,1)S(1)}, bf16[512,1024]{1,0:T(8,128)(2,1)S(1)}, u32[]{:S(2)}, u32[]{:S(2)}) collective-permute-start(bf16[512,1024]{1,0:T(8,128)(2,1)S(1)} %copy-done.15), channel_id=1, source_target_pairs={{0,16},{16,0},{1,17},{17,1},{2,18},{18,2},{3,19},{19,3},{4,20},{20... | collective-permute-start | bytes 3145736 | tf_op jit(solution)/shard_map/ppermute | solution.py:276
  135.2 3.8 %shard_map.85 = (bf16[512,512]{1,0:T(8,128)(2,1)S(1)}, bf16[512,512]{1,0:T(8,128)(2,1)S(1)}) custom-call(s32[3]{0:T(128)S(1)} %pad_add_fusion.refs_0_, bf16[512,512]{1,0:T(8,128)(2,1)S(1)} %get-tuple-element.34.refs_1_, bf16[512,512]{1,0:T(8,128)(2,1)S(1)} %collective-permute-done.2.refs_2_, bf16[512,512]{1,0:T(8,128)(2,1)} %collective-permute-done.3.refs_3_, ...), custom_call_target="tpu_custom_call" | custom-call | flops 1073741824 | bytes 4194304 | tf_op jit(solution)/shard_map/pallas_call | solution.py:219
  142.1 2.7 %collective-permute-start.12 = (bf16[512,512]{1,0:T(8,128)(2,1)S(1)}, bf16[512,512]{1,0:T(8,128)(2,1)S(1)}, u32[]{:S(2)}, u32[]{:S(2)}) collective-permute-start(bf16[512,512]{1,0:T(8,128)(2,1)S(1)} %get-tuple-element.42), channel_id=1, source_target_pairs={{2,1},{3,2},{6,5},{7,6},{10,9},{11,10},{14,13},{15,14},{18,17},{19... | collective-permute-start | bytes 1572872 | tf_op jit(solution)/shard_map/ppermute | solution.py:318
  144.8 5.2 %shard_map.94 = (bf16[512,512]{1,0:T(8,128)(2,1)S(1)}, bf16[512,512]{1,0:T(8,128)(2,1)S(1)}) custom-call(s32[3]{0:T(128)S(1)} %pad_add_fusion.refs_0_, bf16[512,512]{1,0:T(8,128)(2,1)S(1)} %copy-done.3, bf16[512,512]{1,0:T(8,128)(2,1)S(1)} %copy-done.5, bf16[512,512]{1,0:T(8,128)(2,1)} %collective-permute-done.25.refs_3_, ...), custom_call_target="tpu_custom_call" | custom-call | flops 1073741824 | bytes 4194304 | tf_op jit(solution)/shard_map/pallas_call | solution.py:219
  150.0 2.1 %collective-permute-start.31 = (bf16[512,512]{1,0:T(8,128)(2,1)S(1)}, bf16[512,512]{1,0:T(8,128)(2,1)S(1)}, u32[]{:S(2)}, u32[]{:S(2)}) collective-permute-start(bf16[512,512]{1,0:T(8,128)(2,1)S(1)} %get-tuple-element.57), channel_id=1, source_target_pairs={{0,1},{1,2},{2,3},{4,5},{5,6},{6,7},{8,9},{9,10},{10,11},{12,13},{... | collective-permute-start | bytes 1572872 | tf_op jit(solution)/shard_map/ppermute | solution.py:317
  153.4 2.5 %collective-permute-start.32 = (bf16[512,512]{1,0:T(8,128)(2,1)S(1)}, bf16[512,512]{1,0:T(8,128)(2,1)S(1)}, u32[]{:S(2)}, u32[]{:S(2)}) collective-permute-start(bf16[512,512]{1,0:T(8,128)(2,1)S(1)} %get-tuple-element.58), channel_id=1, source_target_pairs={{1,0},{2,1},{3,2},{5,4},{6,5},{7,6},{9,8},{10,9},{11,10},{13,12},{... | collective-permute-start | bytes 1572872 | tf_op jit(solution)/shard_map/ppermute | solution.py:318
  155.9 5.2 %shard_map.90 = (bf16[512,512]{1,0:T(8,128)(2,1)S(1)}, bf16[512,512]{1,0:T(8,128)(2,1)S(1)}) custom-call(s32[3]{0:T(128)S(1)} %pad_add_fusion.refs_0_, bf16[512,512]{1,0:T(8,128)(2,1)S(1)} %get-tuple-element.45.refs_1_, bf16[512,512]{1,0:T(8,128)(2,1)} %collective-permute-done.15.refs_2_, bf16[512,512]{1,0:T(8,128)(2,1)} %collective-permute-done.16.refs_3_, ...), custom_call_target="tpu_custom_call" | custom-call | flops 1073741824 | bytes 4194304 | tf_op jit(solution)/shard_map/pallas_call | solution.py:219
  161.1 2.2 %collective-permute-start.22 = (bf16[512,512]{1,0:T(8,128)(2,1)S(1)}, bf16[512,512]{1,0:T(8,128)(2,1)S(1)}, u32[]{:S(2)}, u32[]{:S(2)}) collective-permute-start(bf16[512,512]{1,0:T(8,128)(2,1)S(1)} %get-tuple-element.50), channel_id=1, source_target_pairs={{0,1},{1,2},{2,3},{4,5},{5,6},{6,7},{8,9},{9,10},{10,11},{12,13},{... | collective-permute-start | bytes 1572872 | tf_op jit(solution)/shard_map/ppermute | solution.py:317
  164.6 2.3 %collective-permute-start.23 = (bf16[512,512]{1,0:T(8,128)(2,1)S(1)}, bf16[512,512]{1,0:T(8,128)(2,1)S(1)}, u32[]{:S(2)}, u32[]{:S(2)}) collective-permute-start(bf16[512,512]{1,0:T(8,128)(2,1)S(1)} %get-tuple-element.51), channel_id=1, source_target_pairs={{1,0},{2,1},{3,2},{5,4},{6,5},{7,6},{9,8},{10,9},{11,10},{13,12},{... | collective-permute-start | bytes 1572872 | tf_op jit(solution)/shard_map/ppermute | solution.py:318
  167.0 5.0 %shard_map.86 = (bf16[512,512]{1,0:T(8,128)(2,1)S(1)}, bf16[512,512]{1,0:T(8,128)(2,1)S(1)}) custom-call(s32[3]{0:T(128)S(1)} %pad_add_fusion.refs_0_, bf16[512,512]{1,0:T(8,128)(2,1)S(1)} %get-tuple-element.34.refs_1_, bf16[512,512]{1,0:T(8,128)(2,1)S(1)} %collective-permute-done.2.refs_2_, bf16[512,512]{1,0:T(8,128)(2,1)} %collective-permute-done.3.refs_3_, ...), custom_call_target="tpu_custom_call" | custom-call | flops 1073741824 | bytes 4194304 | tf_op jit(solution)/shard_map/pallas_call | solution.py:219
  172.0 2.4 %collective-permute-start.13 = (bf16[512,512]{1,0:T(8,128)(2,1)S(1)}, bf16[512,512]{1,0:T(8,128)(2,1)S(1)}, u32[]{:S(2)}, u32[]{:S(2)}) collective-permute-start(bf16[512,512]{1,0:T(8,128)(2,1)S(1)} %get-tuple-element.43), channel_id=1, source_target_pairs={{0,1},{1,2},{2,3},{4,5},{5,6},{6,7},{8,9},{9,10},{10,11},{12,13},{... | collective-permute-start | bytes 1572872 | tf_op jit(solution)/shard_map/ppermute | solution.py:317
  177.9 3.9 %shard_map.95 = bf16[512,512]{1,0:T(8,128)(2,1)S(1)} custom-call(s32[3]{0:T(128)S(1)} %pad_add_fusion.refs_0_, bf16[512,512]{1,0:T(8,128)(2,1)S(1)} %copy-done.3, bf16[512,512]{1,0:T(8,128)(2,1)S(1)} %copy-done.5, bf16[512,512]{1,0:T(8,128)(2,1)} %collective-permute-done.25.refs_3_, bf16[512,512]{1,0:T(8,128)(2,1)} %collective-permute-done.26.refs_4_, ...), custom_call_target="tpu_custom_call" | custom-call | flops 1073741824 | bytes 4194304 | tf_op jit(solution)/shard_map/pallas_call | solution.py:219
  181.8 5.3 %collective-permute-done.23.refs_8_ = bf16[512,512]{1,0:T(8,128)(2,1)S(1)} collective-permute-done((bf16[512,512]{1,0:T(8,128)(2,1)S(1)}, bf16[512,512]{1,0:T(8,128)(2,1)S(1)}, u32[]{:S(2)}, u32[]{:S(2)}) %collective-permute-start.23) | collective-permute-done | bytes 524320 | tf_op jit(solution)/shard_map/ppermute | solution.py:318
  187.1 3.9 %shard_map.91 = bf16[512,512]{1,0:T(8,128)(2,1)S(1)} custom-call(s32[3]{0:T(128)S(1)} %pad_add_fusion.refs_0_, bf16[512,512]{1,0:T(8,128)(2,1)S(1)} %get-tuple-element.45.refs_1_, bf16[512,512]{1,0:T(8,128)(2,1)} %collective-permute-done.15.refs_2_, bf16[512,512]{1,0:T(8,128)(2,1)} %collective-permute-done.16.refs_3_, ...), custom_call_target="tpu_custom_call" | custom-call | flops 1073741824 | bytes 4194304 | tf_op jit(solution)/shard_map/pallas_call | solution.py:219
  191.0 6.4 %collective-permute-done.14.refs_8_ = bf16[512,512]{1,0:T(8,128)(2,1)S(1)} collective-permute-done((bf16[512,512]{1,0:T(8,128)(2,1)S(1)}, bf16[512,512]{1,0:T(8,128)(2,1)S(1)}, u32[]{:S(2)}, u32[]{:S(2)}) %collective-permute-start.14) | collective-permute-done | bytes 524320 | tf_op jit(solution)/shard_map/ppermute | solution.py:318
  197.4 3.7 %shard_map.87 = bf16[512,512]{1,0:T(8,128)(2,1)S(1)} custom-call(s32[3]{0:T(128)S(1)} %pad_add_fusion.refs_0_, bf16[512,512]{1,0:T(8,128)(2,1)S(1)} %get-tuple-element.34.refs_1_, bf16[512,512]{1,0:T(8,128)(2,1)S(1)} %collective-permute-done.2.refs_2_, bf16[512,512]{1,0:T(8,128)(2,1)} %collective-permute-done.3.refs_3_, ...), custom_call_target="tpu_custom_call" | custom-call | flops 1073741824 | bytes 4194304 | tf_op jit(solution)/shard_map/pallas_call | solution.py:219
  (100 shorter events, 51.7 us)
Async XLA Ops:
  0.8 9.7 %collective-permute-start = (bf16[1,48,512]{2,1,0:T(8,128)(2,1)S(1)}, bf16[1,48,512]{2,1,0:T(8,128)(2,1)S(1)}, u32[]{:S(2)}, u32[]{:S(2)}) collective-permute-start(bf16[1,48,512]{2,1,0:T(8,128)(2,1)S(1)} %get-tuple-element.64), channel_id=1, source_target_pairs={{0,16},{1,17},{2,18},{3,19},{4,20},{5,21},{6,22},{7,23},{8,24},{9,... | collective-permute-start | bytes 147464 | tf_op jit(solution)/shard_map/ppermute | solution.py:250
  17.4 19.7 %all-to-all-start = ((bf16[16,48,384]{2,1,0:T(8,128)(2,1)}), bf16[16,48,384]{2,1,0:T(8,128)(2,1)S(1)}, u32[]{:S(2)}, u32[]{:S(2)}) async-start(bf16[16,48,384]{2,1,0:T(8,128)(2,1)} %get-tuple-element.33), calls=%async_computation | async-start | bytes 1179648 | tf_op jit(solution)/shard_map/all_to_all | solution.py:292
  27.8 26.3 %collective-permute-start.5 = (bf16[512,1024]{1,0:T(8,128)(2,1)}, bf16[512,1024]{1,0:T(8,128)(2,1)S(1)}, u32[]{:S(2)}, u32[]{:S(2)}) collective-permute-start(bf16[512,1024]{1,0:T(8,128)(2,1)} %get-tuple-element.35), channel_id=1, source_target_pairs={{0,16},{16,0},{1,17},{17,1},{2,18},{18,2},{3,19},{19,3},{4,20},{20... | collective-permute-start | bytes 3145736 | tf_op jit(solution)/shard_map/ppermute | solution.py:276
  45.6 13.7 %collective-permute-start.25 = (bf16[512,512]{1,0:T(8,128)(2,1)S(1)}, bf16[512,512]{1,0:T(8,128)(2,1)}, u32[]{:S(2)}, u32[]{:S(2)}) collective-permute-start(bf16[512,512]{1,0:T(8,128)(2,1)S(1)} %get-tuple-element.52.refs_1_), channel_id=1, source_target_pairs={{0,8},{4,12},{8,0},{12,4},{1,9},{5,13},{9,1},{13,5},{2,10},{6,14},... | collective-permute-start | bytes 1572872 | tf_op jit(solution)/shard_map/ppermute | solution.py:305
  54.1 32.2 %collective-permute-start.6 = (bf16[512,1024]{1,0:T(8,128)(2,1)}, bf16[512,1024]{1,0:T(8,128)(2,1)S(1)}, u32[]{:S(2)}, u32[]{:S(2)}) collective-permute-start(bf16[512,1024]{1,0:T(8,128)(2,1)} %get-tuple-element.36), channel_id=1, source_target_pairs={{0,16},{16,0},{1,17},{17,1},{2,18},{18,2},{3,19},{19,3},{4,20},{20... | collective-permute-start | bytes 3145736 | tf_op jit(solution)/shard_map/ppermute | solution.py:276
  56.7 14.8 %collective-permute-start.16 = (bf16[512,512]{1,0:T(8,128)(2,1)S(1)}, bf16[512,512]{1,0:T(8,128)(2,1)}, u32[]{:S(2)}, u32[]{:S(2)}) collective-permute-start(bf16[512,512]{1,0:T(8,128)(2,1)S(1)} %get-tuple-element.45.refs_1_), channel_id=1, source_target_pairs={{0,8},{4,12},{8,0},{12,4},{1,9},{5,13},{9,1},{13,5},{2,10},{6,14},... | collective-permute-start | bytes 1572872 | tf_op jit(solution)/shard_map/ppermute | solution.py:305
  57.2 25.1 %collective-permute-start.3 = (bf16[512,512]{1,0:T(8,128)(2,1)S(1)}, bf16[512,512]{1,0:T(8,128)(2,1)}, u32[]{:S(2)}, u32[]{:S(2)}) collective-permute-start(bf16[512,512]{1,0:T(8,128)(2,1)S(1)} %get-tuple-element.34.refs_1_), channel_id=1, source_target_pairs={{0,8},{4,12},{8,0},{12,4},{1,9},{5,13},{9,1},{13,5},{2,10},{6,14},... | collective-permute-start | bytes 1572872 | tf_op jit(solution)/shard_map/ppermute | solution.py:305
  59.3 23.1 %collective-permute-start.26 = (bf16[512,512]{1,0:T(8,128)(2,1)}, bf16[512,512]{1,0:T(8,128)(2,1)}, u32[]{:S(2)}, u32[]{:S(2)}) collective-permute-start(bf16[512,512]{1,0:T(8,128)(2,1)} %collective-permute-done.25.refs_3_), channel_id=1, source_target_pairs={{0,4},{4,0},{8,12},{12,8},{1,5},{5,1},{9,13},{13,9},{2,6},{6,2},{1... | collective-permute-start | bytes 1572872 | tf_op jit(solution)/shard_map/ppermute | solution.py:307
  60.1 27.0 %collective-permute-start.15 = (bf16[512,512]{1,0:T(8,128)(2,1)S(1)}, bf16[512,512]{1,0:T(8,128)(2,1)}, u32[]{:S(2)}, u32[]{:S(2)}) collective-permute-start(bf16[512,512]{1,0:T(8,128)(2,1)S(1)} %get-tuple-element.45.refs_1_), channel_id=1, source_target_pairs={{0,4},{4,0},{8,12},{12,8},{1,5},{5,1},{9,13},{13,9},{2,6},{6,2},{1... | collective-permute-start | bytes 1572872 | tf_op jit(solution)/shard_map/ppermute | solution.py:306
  71.5 20.3 %collective-permute-start.2 = (bf16[512,512]{1,0:T(8,128)(2,1)S(1)}, bf16[512,512]{1,0:T(8,128)(2,1)S(1)}, u32[]{:S(2)}, u32[]{:S(2)}) collective-permute-start(bf16[512,512]{1,0:T(8,128)(2,1)S(1)} %get-tuple-element.34.refs_1_), channel_id=1, source_target_pairs={{0,4},{4,0},{8,12},{12,8},{1,5},{5,1},{9,13},{13,9},{2,6},{6,2},{1... | collective-permute-start | bytes 1572872 | tf_op jit(solution)/shard_map/ppermute | solution.py:306
  82.4 6.9 %collective-permute-start.17 = (bf16[512,512]{1,0:T(8,128)(2,1)}, bf16[512,512]{1,0:T(8,128)(2,1)S(1)}, u32[]{:S(2)}, u32[]{:S(2)}) collective-permute-start(bf16[512,512]{1,0:T(8,128)(2,1)} %collective-permute-done.16.refs_3_), channel_id=1, source_target_pairs={{0,4},{4,0},{8,12},{12,8},{1,5},{5,1},{9,13},{13,9},{2,6},{6,2},{1... | collective-permute-start | bytes 1572872 | tf_op jit(solution)/shard_map/ppermute | solution.py:307
  82.4 10.1 %collective-permute-start.4 = (bf16[512,512]{1,0:T(8,128)(2,1)}, bf16[512,512]{1,0:T(8,128)(2,1)S(1)}, u32[]{:S(2)}, u32[]{:S(2)}) collective-permute-start(bf16[512,512]{1,0:T(8,128)(2,1)} %collective-permute-done.3.refs_3_), channel_id=1, source_target_pairs={{0,4},{4,0},{8,12},{12,8},{1,5},{5,1},{9,13},{13,9},{2,6},{6,2},{1... | collective-permute-start | bytes 1572872 | tf_op jit(solution)/shard_map/ppermute | solution.py:307
  86.4 8.7 %collective-permute-start.27 = (bf16[512,512]{1,0:T(8,128)(2,1)S(1)}, bf16[512,512]{1,0:T(8,128)(2,1)S(1)}, u32[]{:S(2)}, u32[]{:S(2)}) collective-permute-start(bf16[512,512]{1,0:T(8,128)(2,1)S(1)} %get-tuple-element.53), channel_id=1, source_target_pairs={{0,1},{4,5},{8,9},{12,13},{16,17},{20,21},{24,25},{28,29}} | collective-permute-start | bytes 1572872 | tf_op jit(solution)/shard_map/ppermute | solution.py:317
  87.1 39.8 %collective-permute-start.7 = (bf16[512,1024]{1,0:T(8,128)(2,1)S(1)}, bf16[512,1024]{1,0:T(8,128)(2,1)S(1)}, u32[]{:S(2)}, u32[]{:S(2)}) collective-permute-start(bf16[512,1024]{1,0:T(8,128)(2,1)S(1)} %copy-done.16), channel_id=1, source_target_pairs={{0,16},{16,0},{1,17},{17,1},{2,18},{18,2},{3,19},{19,3},{4,20},{20... | collective-permute-start | bytes 3145736 | tf_op jit(solution)/shard_map/ppermute | solution.py:276
  89.2 19.2 %collective-permute-start.28 = (bf16[512,512]{1,0:T(8,128)(2,1)S(1)}, bf16[512,512]{1,0:T(8,128)(2,1)S(1)}, u32[]{:S(2)}, u32[]{:S(2)}) collective-permute-start(bf16[512,512]{1,0:T(8,128)(2,1)S(1)} %get-tuple-element.54), channel_id=1, source_target_pairs={{3,2},{7,6},{11,10},{15,14},{19,18},{23,22},{27,26},{31,30}} | collective-permute-start | bytes 1572872 | tf_op jit(solution)/shard_map/ppermute | solution.py:318
  91.8 21.8 %collective-permute-start.18 = (bf16[512,512]{1,0:T(8,128)(2,1)S(1)}, bf16[512,512]{1,0:T(8,128)(2,1)S(1)}, u32[]{:S(2)}, u32[]{:S(2)}) collective-permute-start(bf16[512,512]{1,0:T(8,128)(2,1)S(1)} %get-tuple-element.46), channel_id=1, source_target_pairs={{0,1},{4,5},{8,9},{12,13},{16,17},{20,21},{24,25},{28,29}} | collective-permute-start | bytes 1572872 | tf_op jit(solution)/shard_map/ppermute | solution.py:317
  92.5 27.1 %collective-permute-start.19 = (bf16[512,512]{1,0:T(8,128)(2,1)S(1)}, bf16[512,512]{1,0:T(8,128)(2,1)S(1)}, u32[]{:S(2)}, u32[]{:S(2)}) collective-permute-start(bf16[512,512]{1,0:T(8,128)(2,1)S(1)} %get-tuple-element.47), channel_id=1, source_target_pairs={{3,2},{7,6},{11,10},{15,14},{19,18},{23,22},{27,26},{31,30}} | collective-permute-start | bytes 1572872 | tf_op jit(solution)/shard_map/ppermute | solution.py:318
  95.1 30.5 %collective-permute-start.9 = (bf16[512,512]{1,0:T(8,128)(2,1)S(1)}, bf16[512,512]{1,0:T(8,128)(2,1)S(1)}, u32[]{:S(2)}, u32[]{:S(2)}) collective-permute-start(bf16[512,512]{1,0:T(8,128)(2,1)S(1)} %get-tuple-element.39), channel_id=1, source_target_pairs={{0,1},{4,5},{8,9},{12,13},{16,17},{20,21},{24,25},{28,29}} | collective-permute-start | bytes 1572872 | tf_op jit(solution)/shard_map/ppermute | solution.py:317
  108.4 24.2 %collective-permute-start.10 = (bf16[512,512]{1,0:T(8,128)(2,1)S(1)}, bf16[512,512]{1,0:T(8,128)(2,1)S(1)}, u32[]{:S(2)}, u32[]{:S(2)}) collective-permute-start(bf16[512,512]{1,0:T(8,128)(2,1)S(1)} %get-tuple-element.40), channel_id=1, source_target_pairs={{3,2},{7,6},{11,10},{15,14},{19,18},{23,22},{27,26},{31,30}} | collective-permute-start | bytes 1572872 | tf_op jit(solution)/shard_map/ppermute | solution.py:318
  113.7 25.3 %collective-permute-start.29 = (bf16[512,512]{1,0:T(8,128)(2,1)S(1)}, bf16[512,512]{1,0:T(8,128)(2,1)S(1)}, u32[]{:S(2)}, u32[]{:S(2)}) collective-permute-start(bf16[512,512]{1,0:T(8,128)(2,1)S(1)} %get-tuple-element.55), channel_id=1, source_target_pairs={{0,1},{1,2},{4,5},{5,6},{8,9},{9,10},{12,13},{13,14},{16,17},{17,1... | collective-permute-start | bytes 1572872 | tf_op jit(solution)/shard_map/ppermute | solution.py:317
  119.7 22.5 %collective-permute-start.30 = (bf16[512,512]{1,0:T(8,128)(2,1)S(1)}, bf16[512,512]{1,0:T(8,128)(2,1)S(1)}, u32[]{:S(2)}, u32[]{:S(2)}) collective-permute-start(bf16[512,512]{1,0:T(8,128)(2,1)S(1)} %get-tuple-element.56), channel_id=1, source_target_pairs={{2,1},{3,2},{6,5},{7,6},{10,9},{11,10},{14,13},{15,14},{18,17},{19... | collective-permute-start | bytes 1572872 | tf_op jit(solution)/shard_map/ppermute | solution.py:318
  125.6 24.4 %collective-permute-start.20 = (bf16[512,512]{1,0:T(8,128)(2,1)S(1)}, bf16[512,512]{1,0:T(8,128)(2,1)S(1)}, u32[]{:S(2)}, u32[]{:S(2)}) collective-permute-start(bf16[512,512]{1,0:T(8,128)(2,1)S(1)} %get-tuple-element.48), channel_id=1, source_target_pairs={{0,1},{1,2},{4,5},{5,6},{8,9},{9,10},{12,13},{13,14},{16,17},{17,1... | collective-permute-start | bytes 1572872 | tf_op jit(solution)/shard_map/ppermute | solution.py:317
  127.0 26.4 %collective-permute-start.21 = (bf16[512,512]{1,0:T(8,128)(2,1)S(1)}, bf16[512,512]{1,0:T(8,128)(2,1)S(1)}, u32[]{:S(2)}, u32[]{:S(2)}) collective-permute-start(bf16[512,512]{1,0:T(8,128)(2,1)S(1)} %get-tuple-element.49), channel_id=1, source_target_pairs={{2,1},{3,2},{6,5},{7,6},{10,9},{11,10},{14,13},{15,14},{18,17},{19... | collective-permute-start | bytes 1572872 | tf_op jit(solution)/shard_map/ppermute | solution.py:318
  132.7 45.2 %collective-permute-start.8 = (bf16[512,1024]{1,0:T(8,128)(2,1)S(1)}, bf16[512,1024]{1,0:T(8,128)(2,1)S(1)}, u32[]{:S(2)}, u32[]{:S(2)}) collective-permute-start(bf16[512,1024]{1,0:T(8,128)(2,1)S(1)} %copy-done.15), channel_id=1, source_target_pairs={{0,16},{16,0},{1,17},{17,1},{2,18},{18,2},{3,19},{19,3},{4,20},{20... | collective-permute-start | bytes 3145736 | tf_op jit(solution)/shard_map/ppermute | solution.py:276
  139.0 22.1 %collective-permute-start.11 = (bf16[512,512]{1,0:T(8,128)(2,1)S(1)}, bf16[512,512]{1,0:T(8,128)(2,1)S(1)}, u32[]{:S(2)}, u32[]{:S(2)}) collective-permute-start(bf16[512,512]{1,0:T(8,128)(2,1)S(1)} %get-tuple-element.41), channel_id=1, source_target_pairs={{0,1},{1,2},{4,5},{5,6},{8,9},{9,10},{12,13},{13,14},{16,17},{17,1... | collective-permute-start | bytes 1572872 | tf_op jit(solution)/shard_map/ppermute | solution.py:317
  142.1 22.5 %collective-permute-start.12 = (bf16[512,512]{1,0:T(8,128)(2,1)S(1)}, bf16[512,512]{1,0:T(8,128)(2,1)S(1)}, u32[]{:S(2)}, u32[]{:S(2)}) collective-permute-start(bf16[512,512]{1,0:T(8,128)(2,1)S(1)} %get-tuple-element.42), channel_id=1, source_target_pairs={{2,1},{3,2},{6,5},{7,6},{10,9},{11,10},{14,13},{15,14},{18,17},{19... | collective-permute-start | bytes 1572872 | tf_op jit(solution)/shard_map/ppermute | solution.py:318
  150.0 21.9 %collective-permute-start.31 = (bf16[512,512]{1,0:T(8,128)(2,1)S(1)}, bf16[512,512]{1,0:T(8,128)(2,1)S(1)}, u32[]{:S(2)}, u32[]{:S(2)}) collective-permute-start(bf16[512,512]{1,0:T(8,128)(2,1)S(1)} %get-tuple-element.57), channel_id=1, source_target_pairs={{0,1},{1,2},{2,3},{4,5},{5,6},{6,7},{8,9},{9,10},{10,11},{12,13},{... | collective-permute-start | bytes 1572872 | tf_op jit(solution)/shard_map/ppermute | solution.py:317
  153.4 22.5 %collective-permute-start.32 = (bf16[512,512]{1,0:T(8,128)(2,1)S(1)}, bf16[512,512]{1,0:T(8,128)(2,1)S(1)}, u32[]{:S(2)}, u32[]{:S(2)}) collective-permute-start(bf16[512,512]{1,0:T(8,128)(2,1)S(1)} %get-tuple-element.58), channel_id=1, source_target_pairs={{1,0},{2,1},{3,2},{5,4},{6,5},{7,6},{9,8},{10,9},{11,10},{13,12},{... | collective-permute-start | bytes 1572872 | tf_op jit(solution)/shard_map/ppermute | solution.py:318
  161.1 20.7 %collective-permute-start.22 = (bf16[512,512]{1,0:T(8,128)(2,1)S(1)}, bf16[512,512]{1,0:T(8,128)(2,1)S(1)}, u32[]{:S(2)}, u32[]{:S(2)}) collective-permute-start(bf16[512,512]{1,0:T(8,128)(2,1)S(1)} %get-tuple-element.50), channel_id=1, source_target_pairs={{0,1},{1,2},{2,3},{4,5},{5,6},{6,7},{8,9},{9,10},{10,11},{12,13},{... | collective-permute-start | bytes 1572872 | tf_op jit(solution)/shard_map/ppermute | solution.py:317
  164.6 22.5 %collective-permute-start.23 = (bf16[512,512]{1,0:T(8,128)(2,1)S(1)}, bf16[512,512]{1,0:T(8,128)(2,1)S(1)}, u32[]{:S(2)}, u32[]{:S(2)}) collective-permute-start(bf16[512,512]{1,0:T(8,128)(2,1)S(1)} %get-tuple-element.51), channel_id=1, source_target_pairs={{1,0},{2,1},{3,2},{5,4},{6,5},{7,6},{9,8},{10,9},{11,10},{13,12},{... | collective-permute-start | bytes 1572872 | tf_op jit(solution)/shard_map/ppermute | solution.py:318
  172.0 19.0 %collective-permute-start.13 = (bf16[512,512]{1,0:T(8,128)(2,1)S(1)}, bf16[512,512]{1,0:T(8,128)(2,1)S(1)}, u32[]{:S(2)}, u32[]{:S(2)}) collective-permute-start(bf16[512,512]{1,0:T(8,128)(2,1)S(1)} %get-tuple-element.43), channel_id=1, source_target_pairs={{0,1},{1,2},{2,3},{4,5},{5,6},{6,7},{8,9},{9,10},{10,11},{12,13},{... | collective-permute-start | bytes 1572872 | tf_op jit(solution)/shard_map/ppermute | solution.py:317
  175.8 21.5 %collective-permute-start.14 = (bf16[512,512]{1,0:T(8,128)(2,1)S(1)}, bf16[512,512]{1,0:T(8,128)(2,1)S(1)}, u32[]{:S(2)}, u32[]{:S(2)}) collective-permute-start(bf16[512,512]{1,0:T(8,128)(2,1)S(1)} %get-tuple-element.44), channel_id=1, source_target_pairs={{1,0},{2,1},{3,2},{5,4},{6,5},{7,6},{9,8},{10,9},{11,10},{13,12},{... | collective-permute-start | bytes 1572872 | tf_op jit(solution)/shard_map/ppermute | solution.py:318
  (21 other events, 90.5 us)

commit v2 on v1

v2 whole, which is shorter than its diff:
```python
import functools
import jax
import jax.numpy as jnp
import numpy as np
from jax import lax
from jax.experimental import pallas as pl
from jax.experimental.pallas import tpu as pltpu
from jax.sharding import PartitionSpec as P

SMEM = pltpu.SMEM
HBM = pltpu.HBM
NT = (((1,), (1,)), ((), ()))
SPLIT = (2, 1)
LIMIT = 60 * 1024 * 1024
HOP_LIMIT = 16 * 1024 * 1024


def takes(microseconds):
    return pl.CostEstimate(flops=int(microseconds * 0.5e9), bytes_accessed=0, transcendentals=0)


TAIL = 16


def line_steps(size):
    order = []
    for c in range(size):
        row = []
        for t in range(1, size):
            if c <= t - 1:
                row.append(c + size - t)
            if c >= size - t:
                row.append(c - size + t)
        row.append(c)
        order.append(row)
    return np.array(order, np.int32)


def slot_of(c, t, size):
    place = 0
    for u in range(1, t):
        place = place + jnp.where(c <= u - 1, 1, 0) + jnp.where(c >= size - u, 1, 0)
    return place


def slots_at(t, size):
    found = set()
    for c in range(size):
        place = 0
        for u in range(1, size):
            for hit in (c <= u - 1, c >= size - u):
                if hit:
                    if u == t:
                        found.add(place)
                    place += 1
        if t == size:
            found.add(size - 1)
    return sorted(found)


def moves(lane, head, fill, spare, on_rim):
    slots = lane.shape[1]
    sub = jnp.broadcast_to(lane, (128, slots)).T[:, 0:1]
    total = jnp.sum((lane >= 0).astype(jnp.float32), axis=1, keepdims=True).astype(jnp.int32)
    in_head = jnp.logical_and(lane >= 0, lane < head)
    head_count = jnp.sum(in_head.astype(jnp.float32), axis=1, keepdims=True).astype(jnp.int32)
    place = lax.broadcasted_iota(jnp.int32, (1, slots), 1)
    tail = jnp.broadcast_to(place + head, (slots, slots))
    wide_sub = jnp.broadcast_to(sub, (slots, slots))
    before = jnp.logical_and(wide_sub >= head, wide_sub < tail).astype(jnp.float32)
    hit = (wide_sub == tail).astype(jnp.float32)
    rank = place - jnp.sum(before, axis=0, keepdims=True).astype(jnp.int32)
    tail_key = jnp.where(jnp.sum(hit, axis=0, keepdims=True) > 0, -2, rank)
    row = lax.broadcasted_iota(jnp.int32, (head, slots), 0)
    wide_lane = jnp.broadcast_to(lane, (head, slots))
    ahead = jnp.logical_and(wide_lane >= 0, wide_lane < row).astype(jnp.float32)
    hits = jnp.max((wide_lane == row).astype(jnp.float32), axis=1, keepdims=True)
    head_key = jnp.where(hits > 0, jnp.sum(ahead, axis=1, keepdims=True).astype(jnp.int32), -1)
    on_rim[...] = hits
    fill[...] = (head_key == tail_key).astype(jnp.float32).astype(jnp.bfloat16)
    slot = lax.broadcasted_iota(jnp.int32, (slots, 1), 0)
    slot_key = jnp.where(slot >= total, slot - total + head_count, -1)
    spare[...] = (slot_key == tail_key).astype(jnp.float32).astype(jnp.bfloat16)
    return sub


def late_mask_kernel(rows_of, cols_of, cells_lane, table, mirror, place, fill, spare, on_rim):
    cell = lax.broadcasted_iota(jnp.int32, place.shape, 0)
    place[...] = (cells_lane[...] == cell).astype(jnp.float32).astype(jnp.bfloat16)
    modes = mirror.shape[1]
    piece = modes // (rows_of * cols_of)
    entry = table[...]
    block = lax.div(entry, modes)
    group = lax.rem(block, rows_of) * cols_of + lax.div(block, rows_of)
    position = group * piece + lax.rem(entry, piece)
    source = lax.broadcasted_iota(jnp.int32, mirror.shape[1:], 0)
    for w in range(mirror.shape[0]):
        mirror[w] = (position[w : w + 1] == source).astype(jnp.float32).astype(jnp.bfloat16)
    moves(cells_lane[...], fill.shape[0], fill, spare, on_rim)


def pick_kernel(where, table, whole, out, sem):
    rows = out.shape[0]
    first = pl.multiple_of(table[where[2], 0] * rows, rows)
    copy = pltpu.make_async_copy(whole.at[pl.ds(first, rows), :], out, sem)
    copy.start()
    copy.wait()


def read_kernel(rows_of, cols_of, count, shards, *refs):
    refs = list(refs)
    dev, before, after, courant, cells_lane = (refs.pop(0) for _ in range(5))
    where, table, whole = (refs.pop(0) for _ in range(3)) if shards else (None, None, None)
    payload, extra = refs.pop(0), refs.pop(0)
    outs = [refs.pop(0) for _ in range(count)]
    parts = [refs.pop(0) for _ in range(shards)]
    read, select, fill, spare, on_rim = (refs.pop(0) for _ in range(5))
    fetches, stores = [], []
    if shards:
        stage, in_sem, out_sem = refs
        rows = stage.shape[1]
        for j in range(shards):
            first = pl.multiple_of(table[where[2], j + 1] * rows, rows)
            fetches.append(
                pltpu.make_async_copy(whole.at[pl.ds(first, rows), :], stage.at[j], in_sem.at[j])
            )
            stores.append(pltpu.make_async_copy(stage.at[j], parts[j], out_sem.at[j]))
    for copy in fetches:
        copy.start()
    sub = moves(cells_lane[...], fill.shape[0], fill, spare, on_rim)
    cell = lax.broadcasted_iota(jnp.int32, select.shape, 1)
    select[...] = (sub == cell).astype(jnp.float32).astype(jnp.bfloat16)
    width_x, width_y, modes = dev.shape
    speed = courant[...]
    reach = jnp.abs(speed)
    ahead = speed > 0
    a = jnp.broadcast_to(reach[0:1], (width_y, modes))
    b = jnp.broadcast_to(reach[1:2], (width_y, modes))
    ahead_x = jnp.broadcast_to(ahead[0:1], (width_y, modes))
    ahead_y = jnp.broadcast_to(ahead[1:2], (width_y, modes))

    def one(x, low, high):
        center = dev[x].astype(jnp.float32)
        ux = jnp.where(ahead_x, low.astype(jnp.float32), high.astype(jnp.float32))
        along = (1.0 - a) * center + a * ux
        shifted = jnp.where(ahead_y, pltpu.roll(along, 1, 0), pltpu.roll(along, width_y - 1, 0))
        read[pl.ds(pl.multiple_of(x * width_y, 16), width_y), :] = (
            (1.0 - b) * along + b * shifted
        ).astype(read.dtype)

    one(0, before[0], dev[1])

    def body(x, carry):
        one(x, dev[x - 1], dev[x + 1])
        return carry

    lax.fori_loop(1, width_x - 1, body, 0)
    one(width_x - 1, dev[width_x - 2], after[0])

    for fetch, store in zip(fetches, stores):
        fetch.wait()
        store.start()
    head = read.shape[0] - extra.shape[0]
    tail_rows = read[head:, :]
    first = 0
    for out in outs:
        rows = slice(first, first + out.shape[0])
        first += out.shape[0]
        moved = jnp.dot(fill[rows, :], tail_rows, preferred_element_type=jnp.float32)
        kept = read[rows, :].astype(jnp.float32)
        out[...] = jnp.where(on_rim[rows, :] > 0, moved, kept).astype(out.dtype)
    extra[...] = jnp.dot(spare[...], tail_rows, preferred_element_type=jnp.float32).astype(extra.dtype)

    rim = jnp.dot(select[...], read[...], preferred_element_type=jnp.float32)
    flipped = rim.T
    total = jnp.sum(flipped, axis=0, keepdims=True)
    high = total.astype(jnp.bfloat16).astype(jnp.float32)
    middle = (total - high).astype(jnp.bfloat16).astype(jnp.float32)
    low = total - high - middle
    place = lax.broadcasted_iota(jnp.int32, (TAIL, total.shape[1]), 0)
    tail = jnp.where(place == 0, high, jnp.where(place == 1, middle, jnp.where(place == 2, low, 0.0)))
    tail = tail.astype(jnp.bfloat16)
    piece = modes // (rows_of * cols_of)
    packed = flipped.astype(jnp.bfloat16)
    for r in range(rows_of):
        for c in range(cols_of):
            block = c * rows_of + r
            payload[r * cols_of + c, 0:piece, :] = packed[block * piece : (block + 1) * piece]
            payload[r * cols_of + c, piece : piece + TAIL, :] = tail
    for store in stores:
        store.wait()


def rim_kernel(mode_count, specularity, arrived, mirror, wall, cells_lane, extra, out):
    groups, height, slots = arrived.shape
    piece = height - TAIL
    values = arrived[:, 0:piece, :].reshape(groups * piece, slots).T
    sums = arrived[:, piece:height, :].reshape(groups * TAIL, slots).astype(jnp.float32)
    total = jnp.broadcast_to(jnp.sum(sums, axis=0, keepdims=True), (128, slots)).T
    diffuse = total[:, 0:1] / mode_count
    walls = jnp.broadcast_to(wall[...], (128, slots)).T[:, 0:1]
    share = jnp.zeros(walls.shape, jnp.float32)
    mirrored = jnp.zeros(out.shape, jnp.float32)
    for w in range(mirror.shape[0]):
        share = jnp.where(walls == w, specularity[w], share)
        picked = jnp.dot(values, mirror[w], preferred_element_type=jnp.float32)
        mirrored = jnp.where(walls == w, picked, mirrored)
    emitted = share * mirrored + (1.0 - share) * diffuse
    used = jnp.broadcast_to(cells_lane[...], (128, slots)).T[:, 0:1] >= 0
    out[...] = jnp.where(used, emitted, extra[...].astype(jnp.float32)).astype(out.dtype)


def ends_kernel(fill, *refs):
    parts, ends = refs[:-1], refs[-1]
    total, first = None, 0
    for part in parts:
        rows = slice(first, first + part.shape[0])
        first += part.shape[0]
        moved = lax.dot_general(
            fill[rows, :], part[...], (((0,), (0,)), ((), ())), preferred_element_type=jnp.float32
        )
        total = moved if total is None else total + moved
    ends[...] = total


def merge_kernel(fill, spare, place, on_rim, ends, total, from_left, from_right, *refs):
    parts, out = refs[:-1], refs[-1]
    head = on_rim.shape[0]
    slots = spare.shape[0]
    total = total[...] + from_left[...].astype(jnp.float32) + from_right[...].astype(jnp.float32)
    total = total.astype(jnp.bfloat16)
    kept = total.shape[0] - slots
    last = total[kept:, :]
    parts = [part[...] for part in parts] + [total[:kept, :]]
    tn = (((0,), (0,)), ((), ()))
    back = lax.dot_general(spare[...], last, tn, preferred_element_type=jnp.float32)
    back = back + jnp.dot(place[head:, :], last, preferred_element_type=jnp.float32)
    back = back + lax.dot_general(
        fill[head - kept :, :], parts[-1], tn, preferred_element_type=jnp.float32
    )
    out[head:, :] = (back + ends[...]).astype(out.dtype)
    first = 0
    for part in parts:
        rows = slice(first, first + part.shape[0])
        first += part.shape[0]
        moved = jnp.dot(place[rows, :], last, preferred_element_type=jnp.float32)
        out[rows, :] = jnp.where(on_rim[rows, :] > 0, moved, part.astype(jnp.float32)).astype(out.dtype)


def hop_kernel(t, size, wide, slots, groups, has_recv, *refs):
    refs = list(refs)
    where = refs.pop(0)
    blocks = [[refs.pop(0) for _ in range(4)] for _ in range(groups)]
    own = refs.pop(0) if wide else None
    held = {j: (refs.pop(0), refs.pop(0)) for j in slots}
    final = t == size
    recv = [refs.pop(0), refs.pop(0)] if has_recv else None
    outs = [refs.pop(0)] if final else [refs.pop(0), refs.pop(0)]
    buffer, sem = refs
    s, r, c = where[0], where[1], where[2]
    rows = buffer.shape[1]
    width = blocks[0][0].shape[1]
    if final:
        jobs = [(c, None, size - 1)]
    else:
        first = slot_of(c, t, size)
        goes_right = c <= t - 1
        jobs = [
            (c + size - t, goes_right, first),
            (c - size + t, c >= size - t, first + jnp.where(goes_right, 1, 0)),
        ]

    def fetch(n, d, place):
        for b in range(4):
            source = lax.bitwise_xor(r, b)
            target = buffer.at[n, :, b * width : (b + 1) * width]
            if wide:
                column = pl.multiple_of(source * width, width)
                pltpu.make_async_copy(
                    own.at[pl.ds(pl.multiple_of(d * rows, rows), rows), pl.ds(column, width)],
                    target,
                    sem.at[n],
                ).start()
                continue
            column = pl.multiple_of(lax.bitwise_and(source, 1) * width, width)
            is_own = lax.shift_right_logical(source, 1) == s
            for j, pair in held.items():
                for use, shard in ((is_own, pair[0]), (jnp.logical_not(is_own), pair[1])):

                    @pl.when(jnp.logical_and(use, place == j))
                    def _(shard=shard):
                        pltpu.make_async_copy(shard.at[:, pl.ds(column, width)], target, sem.at[n]).start()

    def multiply(n, out):
        pltpu.make_async_copy(buffer.at[n], buffer.at[n], sem.at[n]).wait()
        first = 0
        for group in blocks:
            rows_here = slice(first, first + group[0].shape[0])
            first += group[0].shape[0]
            total = None
            for b in range(4):
                part = lax.dot_general(
                    group[b][...],
                    buffer[n, :, b * width : (b + 1) * width],
                    NT,
                    preferred_element_type=jnp.float32,
                )
                total = part if total is None else total + part
            if final and has_recv:
                total = total + recv[0][rows_here, :].astype(jnp.float32)
                total = total + recv[1][rows_here, :].astype(jnp.float32)
            elif has_recv:
                total = total + recv[n][rows_here, :].astype(jnp.float32)
            out[rows_here, :] = total.astype(out.dtype)

    for n, (d, valid, place) in enumerate(jobs):
        if valid is None:
            fetch(n, d, place)
        else:
            pl.when(valid)(functools.partial(fetch, n, d, place))
    for n, (d, valid, place) in enumerate(jobs):
        if valid is None:
            multiply(n, outs[n])
        else:
            pl.when(valid)(functools.partial(multiply, n, outs[n]))


def hop(t, size, where, blocks, own, held, recv):
    wide = own is not None
    slots = () if wide else tuple(slots_at(t, size))
    rows = own.shape[0] // size if wide else held[0][0].shape[0]
    cells = sum(group[0].shape[0] for group in blocks)
    width = blocks[0][0].shape[1]
    count = 1 if t == size else 2
    kept = jnp.float32 if t == size and recv is None else jnp.bfloat16
    spec = pl.BlockSpec(memory_space=pltpu.VMEM)
    any_spec = pl.BlockSpec(memory_space=HBM)
    shards = [own] if wide else [shard for j in slots for shard in held[j]]
    operands = [where, *[block for group in blocks for block in group], *shards, *(recv or [])]
    in_specs = [pl.BlockSpec(memory_space=SMEM)] + [spec] * (4 * len(blocks)) + [any_spec] * len(shards)
    in_specs += [spec] * len(recv or [])
    return pl.pallas_call(
        functools.partial(hop_kernel, t, size, wide, slots, len(blocks), recv is not None),
        out_shape=[jax.ShapeDtypeStruct((cells, rows), kept)] * count,
        in_specs=in_specs,
        out_specs=[spec] * count,
        scratch_shapes=[
            pltpu.VMEM((count, rows, 4 * width), jnp.bfloat16),
            pltpu.SemaphoreType.DMA((count,)),
        ],
        compiler_params=pltpu.CompilerParams(vmem_limit_bytes=HOP_LIMIT),
        cost_estimate=takes(2 + cells / 300),
    )(*operands)


def on_device(deviation, courant, collide, hole_cells, hole_wall, specular, specularity):
    n_space, n_row, n_col = (lax.axis_size(name) for name in ("space", "mrow", "mcol"))
    s, r, c = (lax.axis_index(name) for name in ("space", "mrow", "mcol"))
    width_x, width_y, block_len = deviation.shape
    cell_count = width_x * width_y
    slot_count = hole_cells.shape[0]
    wall_count, mode_count = specular.shape
    piece = block_len // (n_row * n_col)
    groups = n_row * n_col
    vmem = pl.BlockSpec()
    hbm = pl.BlockSpec(memory_space=HBM)
    smem = pl.BlockSpec(memory_space=SMEM)
    params = pltpu.CompilerParams(vmem_limit_bytes=LIMIT)
    where = jnp.stack([s, r, c]).astype(jnp.int32)

    up = [(i, i + 1) for i in range(n_space - 1)]
    down = [(j, i) for i, j in up]
    before_layer = lax.ppermute(deviation[-1:], "space", up)
    after_layer = lax.ppermute(deviation[:1], "space", down)

    def after(value, *first):
        return lax.optimization_barrier((value, first))[0]

    def shape(*dims):
        return jax.ShapeDtypeStruct(dims, jnp.bfloat16)

    head = cell_count - slot_count
    sizes = [head * part // sum(SPLIT) for part in SPLIT]
    count = len(sizes)
    lane_cells = hole_cells[None, :]
    wide = n_space != 2
    rows = collide.shape[0] // n_col
    own = lax.all_gather(collide, "space", axis=1, tiled=True) if wide else None
    shards = 0 if wide else n_col - 1
    swap = [(0, 1), (1, 0)]
    held, order, first = [], jnp.asarray(line_steps(n_col)), ()
    if not wide:
        first = pl.pallas_call(
            pick_kernel,
            out_shape=shape(rows, collide.shape[1]),
            in_specs=[smem, smem, hbm],
            out_specs=vmem,
            scratch_shapes=[pltpu.SemaphoreType.DMA],
            compiler_params=params,
            cost_estimate=takes(2),
        )(where, order, collide)
        held.append((first, lax.ppermute(after(first, before_layer, after_layer), "space", swap)))
    payload, extra, *mine = pl.pallas_call(
        functools.partial(read_kernel, n_row, n_col, count, shards),
        out_shape=[shape(groups, piece + TAIL, slot_count), shape(slot_count, block_len)]
        + [shape(size, block_len) for size in sizes]
        + [shape(rows, collide.shape[1])] * shards,
        in_specs=[vmem] * 5 + [smem, smem, hbm][: shards * 3],
        out_specs=[vmem] * (count + 2) + [hbm] * shards,
        scratch_shapes=[
            pltpu.VMEM((cell_count, block_len), jnp.bfloat16),
            pltpu.VMEM((slot_count, cell_count), jnp.bfloat16),
            pltpu.VMEM((head, slot_count), jnp.bfloat16),
            pltpu.VMEM((slot_count, slot_count), jnp.bfloat16),
            pltpu.VMEM((head, 1), jnp.float32),
        ]
        + [
            pltpu.VMEM((shards, rows, collide.shape[1]), jnp.bfloat16),
            pltpu.SemaphoreType.DMA((shards,)),
            pltpu.SemaphoreType.DMA((shards,)),
        ][: shards * 3],
        compiler_params=params,
        cost_estimate=takes(7),
    )(
        deviation,
        before_layer,
        after_layer,
        courant,
        after(lane_cells, first),
        *([] if wide else [where, order, collide]),
    )
    mine, parts = mine[:count], mine[count:]
    for part in parts:
        held.append((part, lax.ppermute(part, "space", swap)))

    flip = [[(i, i ^ bit) for i in range(n_row)] for bit in (1, 2)]
    right = [(i, i + 1) for i in range(n_col - 1)]
    left = [(j, i) for i, j in right]
    far = []
    for value in mine:
        far.append(lax.ppermute(value, "mrow", flip[1]))
    arrived = lax.all_to_all(payload, ("mrow", "mcol"), split_axis=0, concat_axis=0, tiled=True)
    def send(t, value):
        return [
            lax.ppermute(value[0], "mcol", right[:t]),
            lax.ppermute(value[1], "mcol", left[n_col - 1 - t :]),
        ]

    state = {}
    done = ()

    def step(t, n, *ready):
        return hop(t, n_col, after(where, *done, *ready), chunks[n], own, held, state.get(n))

    def gather(n):
        near = lax.ppermute(mine[n], "mrow", flip[0])
        both = lax.ppermute(after(far[n], *done), "mrow", flip[0])
        return [mine[n], near, far[n], both]

    own_table = lax.dynamic_slice_in_dim(specular, (c * n_row + r) * block_len, block_len, 1)
    mirror, place, fill, spare, on_rim = pl.pallas_call(
        functools.partial(late_mask_kernel, n_row, n_col),
        out_shape=[
            shape(wall_count, block_len, block_len),
            shape(cell_count, slot_count),
            shape(head, slot_count),
            shape(slot_count, slot_count),
            jax.ShapeDtypeStruct((head, 1), jnp.float32),
        ],
        in_specs=[vmem] * 2,
        out_specs=[vmem] * 5,
        compiler_params=params,
        cost_estimate=takes(4),
    )(after(lane_cells, extra), own_table)
    far[0] = after(far[0], mirror)
    chunks = [[gather(0)]]
    done = step(1, 0)
    state[0] = send(1, done)
    mine.append(
        pl.pallas_call(
            functools.partial(rim_kernel, mode_count),
            out_shape=shape(slot_count, block_len),
            in_specs=[smem] + [vmem] * 5,
            out_specs=vmem,
            compiler_params=params,
            cost_estimate=takes(4),
        )(specularity, after(arrived, *done), mirror, hole_wall[None, :], lane_cells, extra)
    )
    far.append(lax.ppermute(mine[count], "mrow", flip[1]))
    chunks.append([gather(n) for n in range(1, count + 1)])
    done = step(1, 1, *state[0])
    state[1] = send(1, done)
    outs = []
    for t in range(2, n_col + 1):
        for n in (0, 1):
            if (t, n) == (n_col, 1):
                continue
            done = step(t, n)
            if t == n_col:
                outs.append(done[0])
            else:
                state[n] = send(t, done)
    total = hop(n_col, n_col, after(where, *done), chunks[1], own, held, None)[0]
    ends = pl.pallas_call(
        ends_kernel,
        out_shape=jax.ShapeDtypeStruct((slot_count, rows), jnp.float32),
        in_specs=[vmem] * (1 + len(outs)),
        out_specs=vmem,
        compiler_params=params,
        cost_estimate=takes(2),
    )(fill, *outs)
    out = pl.pallas_call(
        merge_kernel,
        out_shape=shape(cell_count, rows),
        in_specs=[vmem] * (8 + len(outs)),
        out_specs=vmem,
        compiler_params=params,
        cost_estimate=takes(4),
    )(fill, spare, place, on_rim, ends, total, *state[1], *outs)
    return out.reshape(width_x, width_y, rows)


def solution(mesh):
    in_specs = (
        P("space", None, ("mcol", "mrow")),
        P(None, ("mcol", "mrow")),
        P("mrow", ("mcol", "space")),
        P("space"),
        P("space"),
        P(),
        P(),
    )
    out_specs = P("space", None, ("mrow", "mcol"))
    return jax.shard_map(
        on_device, mesh=mesh, in_specs=in_specs, out_specs=out_specs, check_vma=False
    )
```

time: 204 us -> 179 us (0.88)
  waiting for transfers between devices: 67.2 us -> 54.1 us
  Pallas kernels: 49.8 us -> 60.9 us
  local copies, waits for them, and re-layouts: 18.4 us -> 8.85 us
  other arithmetic: 6.44 us -> 0.61 us
  starting transfers between devices: 57.5 us -> 52.4 us
  between operations: 3.11 us -> 0.49 us
    ppermute x33 -> x27, waiting for transfers between devices: 64.9 us -> 48.1 us  [the longest x6 20.9 us: send(): lax.ppermute(value[1], 'mcol', left[n_col - 1 - t:])]
    pallas_call x14, Pallas kernels: 49.8 us -> 60.9 us  [the longest x8 32.9 us: hop(): pl.pallas_call(functools.partial(hop_kernel, t, size, wide, slots, len(bl...]
    unnamed x38 -> x56, local copies, waits for them, and re-layouts: 11.5 us -> 5.55 us
    ppermute x33 -> x27, starting transfers between devices: 51.3 us -> 46.2 us  [the longest x6 19.6 us: send(): lax.ppermute(value[1], 'mcol', left[n_col - 1 - t:])]
    dynamic_slice x2 -> x1, local copies, waits for them, and re-layouts: 5.74 us -> 0.6 us  [on_device(): lax.dynamic_slice_in_dim(specular, (c * n_row + r) * block_len, block_len...]
    convert_element_type x3 -> x0, other arithmetic: 4.03 us -> none  [the longest x1 1.6 us: on_device(): mirror = (positions[:, :, None] == jnp.arange(block_len, dtype=jnp.int32)...]
    all_to_all x1, waiting for transfers between devices: 2.22 us -> 5.95 us  [on_device(): lax.all_to_all(payload, ('mrow', 'mcol'), split_axis=0, concat_axis=0, ti...]
  transfers between devices with their start and end apart: 34 -> 28, of which waited for: 13 -> 13; matrix products, arithmetic and copies ran while one was open for 6% -> 2% of each run, Pallas kernels for 21% -> 27%
where the time goes in v2:
time: 179 us; the launch traced here: 177 us
  Pallas kernels  60.9 us (34%)
  waiting for transfers between devices  54.1 us (30%)
  starting transfers between devices  52.4 us (29%)
  local copies, waits for them, and re-layouts  8.85 us (5%)
    pallas_call x8, Pallas kernels, hop(): pl.pallas_call(functools.partial(hop_kernel, t, size, wide, slots, len(bl...  32.9 us
    ppermute x6, waiting for transfers between devices, send(): lax.ppermute(value[1], 'mcol', left[n_col - 1 - t:])  20.9 us
    ppermute x6, starting transfers between devices, send(): lax.ppermute(value[1], 'mcol', left[n_col - 1 - t:])  19.6 us
    ppermute x2, waiting for transfers between devices, on_device(): far.append(lax.ppermute(value, 'mrow', flip[1]))  11 us
    ppermute x6, starting transfers between devices, send(): lax.ppermute(value[0], 'mcol', right[:t])  8.69 us
    pallas_call x1, Pallas kernels, on_device(): pl.pallas_call(functools.partial(read_kernel, n_row, n_col, count, shards...  7.91 us
    ppermute x1, waiting for transfers between devices, on_device(): far.append(lax.ppermute(mine[count], 'mrow', flip[1]))  7.73 us
    ppermute x3, starting transfers between devices, on_device(): held.append((part, lax.ppermute(part, 'space', swap)))  7.23 us
  transfers between devices with their start and end apart: 28, of which 13 were waited for; matrix products, arithmetic and copies ran while one was open for 2% of the time, Pallas kernels for 27%

profile of v2, /device:TPU:20, one launch (start us, length us, event | category | flops | bytes accessed | tf_op | source)
XLA Modules:
  0.0 177.3 jit_solution(8373176153465675199)
XLA Ops:
  0.9 3.4 %collective-permute-start = (bf16[1,48,512]{2,1,0:T(8,128)(2,1)S(1)}, bf16[1,48,512]{2,1,0:T(8,128)(2,1)S(1)}, u32[]{:S(2)}, u32[]{:S(2)}) collective-permute-start(bf16[1,48,512]{2,1,0:T(8,128)(2,1)S(1)} %get-tuple-element.82), channel_id=1, source_target_pairs={{0,16},{1,17},{2,18},{3,19},{4,20},{5,21},{6,22},{7,23},{8,24},{9,... | collective-permute-start | bytes 147464 | tf_op jit(solution)/shard_map/ppermute | solution.py:373
  7.4 3.0 %shard_map.82.refs_5_.refs_9_ = bf16[512,1024]{1,0:T(8,128)(2,1)} custom-call(s32[3]{0:T(128)} %pad_add_fusion.where.refs_5_.refs_0_, s32[4,4]{1,0:T(4,128)} %constant.23.clone.table.refs_6_, bf16[2048,1024]{1,0:T(8,128)(2,1)} %refs_7_.1), custom_call_target="tpu_custom_call" | custom-call | flops 1000000000 | tf_op jit(solution)/shard_map/pallas_call | solution.py:393
  11.6 7.9 %shard_map.83 = (bf16[16,48,384]{2,1,0:T(8,128)(2,1)}, bf16[384,512]{1,0:T(8,128)(2,1)}, bf16[768,512]{1,0:T(8,128)(2,1)}, bf16[384,512]{1,0:T(8,128)(2,1)}, bf1...) custom-call(bf16[32,48,512]{2,1,0:T(8,128)(2,1)} %refs_0_.1, ...), custom_call_target="tpu_custom_call" | custom-call | flops 3500000000 | tf_op jit(solution)/shard_map/pallas_call | solution.py:403
  20.1 2.6 %collective-permute-start.5 = (bf16[512,1024]{1,0:T(8,128)(2,1)S(1)}, bf16[512,1024]{1,0:T(8,128)(2,1)S(1)}, u32[]{:S(2)}, u32[]{:S(2)}) collective-permute-start(bf16[512,1024]{1,0:T(8,128)(2,1)S(1)} %copy-done.2), channel_id=1, source_target_pairs={{0,16},{16,0},{1,17},{17,1},{2,18},{18,2},{3,19},{19,3},{4,20},{20... | collective-permute-start | bytes 3145736 | tf_op jit(solution)/shard_map/ppermute | solution.py:402
  23.4 4.6 %shard_map.84 = (bf16[4,512,512]{2,1,0:T(8,128)(2,1)}, bf16[1536,384]{1,0:T(8,128)(2,1)}, bf16[1152,384]{1,0:T(8,128)(2,1)}, bf16[384,384]{1,0:T(8,128)(2,1)}, f32[1152,1]{1,0:T(8,128)}) custom-call(s32[1,384]{1,0:T(1,128)} %broadcast_in_dim.6.refs_4_.cells_lane, s32[4,512]{1,0:T(4,128)} %constant_dynamic-slice_fusion.table), custom_call_target="tpu_custom_call" | custom-call | flops 2000000000 | tf_op jit(solution)/shard_map/pallas_call | solution.py:461
  28.0 11.0 %collective-permute-done.3.refs_3_ = bf16[768,512]{1,0:T(8,128)(2,1)} collective-permute-done((bf16[768,512]{1,0:T(8,128)(2,1)}, bf16[768,512]{1,0:T(8,128)(2,1)}, u32[]{:S(2)}, u32[]{:S(2)}) %collective-permute-start.3) | collective-permute-done | bytes 786464 | tf_op jit(solution)/shard_map/ppermute | solution.py:441
  38.9 6.2 %all-to-all-start = ((bf16[16,48,384]{2,1,0:T(8,128)(2,1)}), bf16[16,48,384]{2,1,0:T(8,128)(2,1)}, u32[]{:S(2)}, u32[]{:S(2)}) async-start(bf16[16,48,384]{2,1,0:T(8,128)(2,1)} %get-tuple-element.59), calls=%async_computation | async-start | bytes 1179648 | tf_op jit(solution)/shard_map/all_to_all | solution.py:442
  45.2 2.9 %shard_map.85 = (bf16[768,512]{1,0:T(8,128)(2,1)}, bf16[768,512]{1,0:T(8,128)(2,1)}) custom-call(s32[3]{0:T(128)S(1)} %copy-done.20, bf16[768,512]{1,0:T(8,128)(2,1)S(1)} %copy-done.4, bf16[768,512]{1,0:T(8,128)(2,1)} %collective-permute-done.2.refs_2_, bf16[768,512]{1,0:T(8,128)(2,1)} %collective-permute-done.3.refs_3_, ...), custom_call_target="tpu_custom_call" | custom-call | flops 2280000000 | tf_op jit(solution)/shard_map/pallas_call | solution.py:342
  53.0 5.9 %all-to-all-done.arrived = bf16[16,48,384]{2,1,0:T(8,128)(2,1)} async-done(((bf16[16,48,384]{2,1,0:T(8,128)(2,1)}), bf16[16,48,384]{2,1,0:T(8,128)(2,1)}, u32[]{:S(2)}, u32[]{:S(2)}) %all-to-all-start) | async-done | bytes 589856 | tf_op jit(solution)/shard_map/all_to_all | solution.py:442
  58.9 3.7 %shard_map.86.refs_5_ = bf16[384,512]{1,0:T(8,128)(2,1)} custom-call(f32[4]{0:T(128)} %specularity.1, bf16[16,48,384]{2,1,0:T(8,128)(2,1)} %all-to-all-done.arrived, bf16[4,512,512]{2,1,0:T(8,128)(2,1)} %get-tuple-element.51.mirror, s32[1,384]{1,0:T(1,128)} %broadcast_in_dim.7.wall, s32[1,384]{1,0:T(1,128)} %broadcast_in_dim.6.refs_4_.cells_lane, ...), custom_call_target="tpu_custom_call" | custom-call | flops 2000000000 | tf_op jit(solution)/shard_map/pallas_call | solution.py:480
  63.4 2.4 %collective-permute-start.14 = (bf16[512,1024]{1,0:T(8,128)(2,1)S(1)}, bf16[512,1024]{1,0:T(8,128)(2,1)S(1)}, u32[]{:S(2)}, u32[]{:S(2)}) collective-permute-start(bf16[512,1024]{1,0:T(8,128)(2,1)S(1)} %copy-done.1), channel_id=1, source_target_pairs={{0,16},{16,0},{1,17},{17,1},{2,18},{18,2},{3,19},{19,3},{4,20},{20... | collective-permute-start | bytes 3145736 | tf_op jit(solution)/shard_map/ppermute | solution.py:434
  65.8 7.7 %collective-permute-done.12.refs_7_ = bf16[384,512]{1,0:T(8,128)(2,1)S(1)} collective-permute-done((bf16[384,512]{1,0:T(8,128)(2,1)}, bf16[384,512]{1,0:T(8,128)(2,1)S(1)}, u32[]{:S(2)}, u32[]{:S(2)}) %collective-permute-start.12) | collective-permute-done | bytes 393248 | tf_op jit(solution)/shard_map/ppermute | solution.py:489
  80.9 2.4 %collective-permute-start.17 = (bf16[512,1024]{1,0:T(8,128)(2,1)S(1)}, bf16[512,1024]{1,0:T(8,128)(2,1)S(1)}, u32[]{:S(2)}, u32[]{:S(2)}) collective-permute-start(bf16[512,1024]{1,0:T(8,128)(2,1)S(1)} %copy-done.3), channel_id=1, source_target_pairs={{0,16},{16,0},{1,17},{17,1},{2,18},{18,2},{3,19},{19,3},{4,20},{20... | collective-permute-start | bytes 3145736 | tf_op jit(solution)/shard_map/ppermute | solution.py:434
  83.3 6.4 %collective-permute-done.14.refs_8_.refs_12_.refs_6_.refs_10_ = bf16[512,1024]{1,0:T(8,128)(2,1)S(1)} collective-permute-done((bf16[512,1024]{1,0:T(8,128)(2,1)S(1)}, bf16[512,1024]{1,0:T(8,128)(2,1)S(1)}, u32[]{:S(2)}, u32[]{:S(2)}) %collective-permute-start.14) | collective-permute-done | bytes 1048608 | tf_op jit(solution)/shard_map/ppermute | solution.py:434
  89.7 4.4 %shard_map.88 = (bf16[768,512]{1,0:T(8,128)(2,1)S(1)}, bf16[768,512]{1,0:T(8,128)(2,1)S(1)}) custom-call(s32[3]{0:T(128)S(1)} %copy-done.20, bf16[768,512]{1,0:T(8,128)(2,1)S(1)} %copy-done.5, bf16[768,512]{1,0:T(8,128)(2,1)} %collective-permute-done.2.refs_2_, bf16[768,512]{1,0:T(8,128)(2,1)} %collective-permute-done.3.refs_3_, ...), custom_call_target="tpu_custom_call" | custom-call | flops 2280000000 | tf_op jit(solution)/shard_map/pallas_call | solution.py:342
  95.4 4.7 %collective-permute-start.19 = (bf16[768,512]{1,0:T(8,128)(2,1)S(1)}, bf16[768,512]{1,0:T(8,128)(2,1)S(1)}, u32[]{:S(2)}, u32[]{:S(2)}) collective-permute-start(bf16[768,512]{1,0:T(8,128)(2,1)S(1)} %get-tuple-element.67), channel_id=1, source_target_pairs={{2,1},{3,2},{6,5},{7,6},{10,9},{11,10},{14,13},{15,14},{18,17},{19... | collective-permute-start | bytes 2359304 | tf_op jit(solution)/shard_map/ppermute | solution.py:446
  100.1 4.5 %collective-permute-done.16.refs_14_ = bf16[768,512]{1,0:T(8,128)(2,1)S(1)} collective-permute-done((bf16[768,512]{1,0:T(8,128)(2,1)S(1)}, bf16[768,512]{1,0:T(8,128)(2,1)S(1)}, u32[]{:S(2)}, u32[]{:S(2)}) %collective-permute-start.16) | collective-permute-done | bytes 786464 | tf_op jit(solution)/shard_map/ppermute | solution.py:446
  104.6 3.4 %shard_map.89 = (bf16[768,512]{1,0:T(8,128)(2,1)S(1)}, bf16[768,512]{1,0:T(8,128)(2,1)S(1)}) custom-call(s32[3]{0:T(128)S(1)} %copy-done.20, bf16[384,512]{1,0:T(8,128)(2,1)} %get-tuple-element.57.refs_1_, bf16[384,512]{1,0:T(8,128)(2,1)S(1)} %collective-permute-done.8.refs_2_, bf16[384,512]{1,0:T(8,128)(2,1)} %collective-permute-done.9.refs_3_, ...), custom_call_target="tpu_custom_call" | custom-call | flops 2280000000 | tf_op jit(solution)/shard_map/pallas_call | solution.py:342
  109.3 4.6 %collective-permute-start.21 = (bf16[768,512]{1,0:T(8,128)(2,1)S(1)}, bf16[768,512]{1,0:T(8,128)(2,1)S(1)}, u32[]{:S(2)}, u32[]{:S(2)}) collective-permute-start(bf16[768,512]{1,0:T(8,128)(2,1)S(1)} %get-tuple-element.70), channel_id=1, source_target_pairs={{2,1},{3,2},{6,5},{7,6},{10,9},{11,10},{14,13},{15,14},{18,17},{19... | collective-permute-start | bytes 2359304 | tf_op jit(solution)/shard_map/ppermute | solution.py:446
  113.9 2.4 %collective-permute-start.22 = (bf16[512,1024]{1,0:T(8,128)(2,1)S(1)}, bf16[512,1024]{1,0:T(8,128)(2,1)S(1)}, u32[]{:S(2)}, u32[]{:S(2)}) collective-permute-start(bf16[512,1024]{1,0:T(8,128)(2,1)S(1)} %copy-done.21), channel_id=1, source_target_pairs={{0,16},{16,0},{1,17},{17,1},{2,18},{18,2},{3,19},{19,3},{4,20},{20... | collective-permute-start | bytes 3145736 | tf_op jit(solution)/shard_map/ppermute | solution.py:434
  116.5 5.0 %collective-permute-done.19.refs_10_ = bf16[768,512]{1,0:T(8,128)(2,1)S(1)} collective-permute-done((bf16[768,512]{1,0:T(8,128)(2,1)S(1)}, bf16[768,512]{1,0:T(8,128)(2,1)S(1)}, u32[]{:S(2)}, u32[]{:S(2)}) %collective-permute-start.19) | collective-permute-done | bytes 786464 | tf_op jit(solution)/shard_map/ppermute | solution.py:446
  121.4 6.4 %shard_map.90 = (bf16[768,512]{1,0:T(8,128)(2,1)S(1)}, bf16[768,512]{1,0:T(8,128)(2,1)S(1)}) custom-call(s32[3]{0:T(128)S(1)} %copy-done.20, bf16[768,512]{1,0:T(8,128)(2,1)S(1)} %copy-done.5, bf16[768,512]{1,0:T(8,128)(2,1)} %collective-permute-done.2.refs_2_, bf16[768,512]{1,0:T(8,128)(2,1)} %collective-permute-done.3.refs_3_, ...), custom_call_target="tpu_custom_call" | custom-call | flops 2280000000 | tf_op jit(solution)/shard_map/pallas_call | solution.py:342
  129.8 3.9 %collective-permute-start.24 = (bf16[768,512]{1,0:T(8,128)(2,1)S(1)}, bf16[768,512]{1,0:T(8,128)(2,1)S(1)}, u32[]{:S(2)}, u32[]{:S(2)}) collective-permute-start(bf16[768,512]{1,0:T(8,128)(2,1)S(1)} %get-tuple-element.74), channel_id=1, source_target_pairs={{1,0},{2,1},{3,2},{5,4},{6,5},{7,6},{9,8},{10,9},{11,10},{13,12},{... | collective-permute-start | bytes 2359304 | tf_op jit(solution)/shard_map/ppermute | solution.py:446
  133.7 4.6 %collective-permute-done.21.refs_14_ = bf16[768,512]{1,0:T(8,128)(2,1)S(1)} collective-permute-done((bf16[768,512]{1,0:T(8,128)(2,1)S(1)}, bf16[768,512]{1,0:T(8,128)(2,1)S(1)}, u32[]{:S(2)}, u32[]{:S(2)}) %collective-permute-start.21) | collective-permute-done | bytes 786464 | tf_op jit(solution)/shard_map/ppermute | solution.py:446
  138.3 6.8 %shard_map.91 = (bf16[768,512]{1,0:T(8,128)(2,1)}, bf16[768,512]{1,0:T(8,128)(2,1)}) custom-call(s32[3]{0:T(128)S(1)} %copy-done.20, bf16[384,512]{1,0:T(8,128)(2,1)} %get-tuple-element.57.refs_1_, bf16[384,512]{1,0:T(8,128)(2,1)S(1)} %collective-permute-done.8.refs_2_, bf16[384,512]{1,0:T(8,128)(2,1)} %collective-permute-done.9.refs_3_, ...), custom_call_target="tpu_custom_call" | custom-call | flops 2280000000 | tf_op jit(solution)/shard_map/pallas_call | solution.py:342
  147.1 3.9 %collective-permute-start.26 = (bf16[768,512]{1,0:T(8,128)(2,1)}, bf16[768,512]{1,0:T(8,128)(2,1)}, u32[]{:S(2)}, u32[]{:S(2)}) collective-permute-start(bf16[768,512]{1,0:T(8,128)(2,1)} %get-tuple-element.77), channel_id=1, source_target_pairs={{1,0},{2,1},{3,2},{5,4},{6,5},{7,6},{9,8},{10,9},{11,10},{13,12},{... | collective-permute-start | bytes 2359304 | tf_op jit(solution)/shard_map/ppermute | solution.py:446
  151.1 4.1 %collective-permute-done.24.refs_8_ = bf16[768,512]{1,0:T(8,128)(2,1)S(1)} collective-permute-done((bf16[768,512]{1,0:T(8,128)(2,1)S(1)}, bf16[768,512]{1,0:T(8,128)(2,1)S(1)}, u32[]{:S(2)}, u32[]{:S(2)}) %collective-permute-start.24) | collective-permute-done | bytes 786464 | tf_op jit(solution)/shard_map/ppermute | solution.py:446
  155.1 3.9 %shard_map.92.refs_0_ = bf16[768,512]{1,0:T(8,128)(2,1)S(1)} custom-call(s32[3]{0:T(128)S(1)} %copy-done.20, bf16[768,512]{1,0:T(8,128)(2,1)S(1)} %copy-done.5, bf16[768,512]{1,0:T(8,128)(2,1)} %collective-permute-done.2.refs_2_, bf16[768,512]{1,0:T(8,128)(2,1)} %collective-permute-done.3.refs_3_, bf16[768,512]{1,0:T(8,128)(2,1)} %collective-permute-done.4.refs_4_, ...), custom_call_target="tpu_custom_call" | custom-call | flops 2280000000 | tf_op jit(solution)/shard_map/pallas_call | solution.py:342
  160.0 3.0 %shard_map.93.ends = f32[384,512]{1,0:T(8,128)} custom-call(bf16[1152,384]{1,0:T(8,128)(2,1)} %get-tuple-element.46.fill, bf16[768,512]{1,0:T(8,128)(2,1)} %copy-done.19), custom_call_target="tpu_custom_call" | custom-call | flops 1000000000 | tf_op jit(solution)/shard_map/pallas_call | solution.py:504
  164.3 3.6 %shard_map.94.total = f32[768,512]{1,0:T(8,128)S(1)} custom-call(s32[3]{0:T(128)S(1)} %copy-done.20, bf16[384,512]{1,0:T(8,128)(2,1)} %get-tuple-element.57.refs_1_, bf16[384,512]{1,0:T(8,128)(2,1)S(1)} %copy-done.11, bf16[384,512]{1,0:T(8,128)(2,1)} %collective-permute-done.9.refs_3_, bf16[384,512]{1,0:T(8,128)(2,1)S(1)} %copy-done.15, ...), custom_call_target="tpu_custom_call" | custom-call | flops 2280000000 | tf_op jit(solution)/shard_map/pallas_call | solution.py:342
  169.1 2.5 %collective-permute-done.26.from_right = bf16[768,512]{1,0:T(8,128)(2,1)} collective-permute-done((bf16[768,512]{1,0:T(8,128)(2,1)}, bf16[768,512]{1,0:T(8,128)(2,1)}, u32[]{:S(2)}, u32[]{:S(2)}) %collective-permute-start.26) | collective-permute-done | bytes 786464 | tf_op jit(solution)/shard_map/ppermute | solution.py:446
  171.5 5.8 %shard_map.95 = bf16[1536,512]{1,0:T(8,128)(2,1)} custom-call(bf16[1152,384]{1,0:T(8,128)(2,1)} %get-tuple-element.46.fill, bf16[384,384]{1,0:T(8,128)(2,1)} %get-tuple-element.47.spare, bf16[1536,384]{1,0:T(8,128)(2,1)} %get-tuple-element.48.place, f32[1152,1]{1,0:T(8,128)} %get-tuple-element.49.on_rim, f32[384,512]{1,0:T(8,128)} %shard_map.93.ends, ...), custom_call_target="tpu_custom_call" | custom-call | flops 2000000000 | tf_op jit(solution)/shard_map/pallas_call | solution.py:512
  (99 shorter events, 29.3 us)
Async XLA Ops:
  0.9 9.5 %collective-permute-start = (bf16[1,48,512]{2,1,0:T(8,128)(2,1)S(1)}, bf16[1,48,512]{2,1,0:T(8,128)(2,1)S(1)}, u32[]{:S(2)}, u32[]{:S(2)}) collective-permute-start(bf16[1,48,512]{2,1,0:T(8,128)(2,1)S(1)} %get-tuple-element.82), channel_id=1, source_target_pairs={{0,16},{1,17},{2,18},{3,19},{4,20},{5,21},{6,22},{7,23},{8,24},{9,... | collective-permute-start | bytes 147464 | tf_op jit(solution)/shard_map/ppermute | solution.py:373
  4.3 6.2 %collective-permute-start.1 = (bf16[1,48,512]{2,1,0:T(8,128)(2,1)S(1)}, bf16[1,48,512]{2,1,0:T(8,128)(2,1)S(1)}, u32[]{:S(2)}, u32[]{:S(2)}) collective-permute-start(bf16[1,48,512]{2,1,0:T(8,128)(2,1)S(1)} %get-tuple-element.81), channel_id=1, source_target_pairs={{16,0},{17,1},{18,2},{19,3},{20,4},{21,5},{22,6},{23,7},{24,8},{25... | collective-permute-start | bytes 147464 | tf_op jit(solution)/shard_map/ppermute | solution.py:374
  19.6 19.4 %collective-permute-start.3 = (bf16[768,512]{1,0:T(8,128)(2,1)}, bf16[768,512]{1,0:T(8,128)(2,1)}, u32[]{:S(2)}, u32[]{:S(2)}) collective-permute-start(bf16[768,512]{1,0:T(8,128)(2,1)} %get-tuple-element.50.refs_1_), channel_id=1, source_target_pairs={{0,8},{4,12},{8,0},{12,4},{1,9},{5,13},{9,1},{13,5},{2,10},{6,14},... | collective-permute-start | bytes 2359304 | tf_op jit(solution)/shard_map/ppermute | solution.py:441
  20.1 25.1 %collective-permute-start.5 = (bf16[512,1024]{1,0:T(8,128)(2,1)S(1)}, bf16[512,1024]{1,0:T(8,128)(2,1)S(1)}, u32[]{:S(2)}, u32[]{:S(2)}) collective-permute-start(bf16[512,1024]{1,0:T(8,128)(2,1)S(1)} %copy-done.2), channel_id=1, source_target_pairs={{0,16},{16,0},{1,17},{17,1},{2,18},{18,2},{3,19},{19,3},{4,20},{20... | collective-permute-start | bytes 3145736 | tf_op jit(solution)/shard_map/ppermute | solution.py:402
  23.4 21.8 %collective-permute-start.2 = (bf16[768,512]{1,0:T(8,128)(2,1)}, bf16[768,512]{1,0:T(8,128)(2,1)}, u32[]{:S(2)}, u32[]{:S(2)}) collective-permute-start(bf16[768,512]{1,0:T(8,128)(2,1)} %get-tuple-element.50.refs_1_), channel_id=1, source_target_pairs={{0,4},{4,0},{8,12},{12,8},{1,5},{5,1},{9,13},{13,9},{2,6},{6,2},{1... | collective-permute-start | bytes 2359304 | tf_op jit(solution)/shard_map/ppermute | solution.py:456
  38.9 6.3 %collective-permute-start.4 = (bf16[768,512]{1,0:T(8,128)(2,1)}, bf16[768,512]{1,0:T(8,128)(2,1)}, u32[]{:S(2)}, u32[]{:S(2)}) collective-permute-start(bf16[768,512]{1,0:T(8,128)(2,1)} %collective-permute-done.3.refs_3_), channel_id=1, source_target_pairs={{0,4},{4,0},{8,12},{12,8},{1,5},{5,1},{9,13},{13,9},{2,6},{6,2},{1... | collective-permute-start | bytes 2359304 | tf_op jit(solution)/shard_map/ppermute | solution.py:457
  38.9 20.0 %all-to-all-start = ((bf16[16,48,384]{2,1,0:T(8,128)(2,1)}), bf16[16,48,384]{2,1,0:T(8,128)(2,1)}, u32[]{:S(2)}, u32[]{:S(2)}) async-start(bf16[16,48,384]{2,1,0:T(8,128)(2,1)} %get-tuple-element.59), calls=%async_computation | async-start | bytes 1179648 | tf_op jit(solution)/shard_map/all_to_all | solution.py:442
  48.1 25.4 %collective-permute-start.6 = (bf16[768,512]{1,0:T(8,128)(2,1)}, bf16[768,512]{1,0:T(8,128)(2,1)}, u32[]{:S(2)}, u32[]{:S(2)}) collective-permute-start(bf16[768,512]{1,0:T(8,128)(2,1)} %get-tuple-element.54), channel_id=1, source_target_pairs={{0,1},{4,5},{8,9},{12,13},{16,17},{20,21},{24,25},{28,29}} | collective-permute-start | bytes 2359304 | tf_op jit(solution)/shard_map/ppermute | solution.py:445
  49.7 24.6 %collective-permute-start.7 = (bf16[768,512]{1,0:T(8,128)(2,1)}, bf16[768,512]{1,0:T(8,128)(2,1)}, u32[]{:S(2)}, u32[]{:S(2)}) collective-permute-start(bf16[768,512]{1,0:T(8,128)(2,1)} %get-tuple-element.55), channel_id=1, source_target_pairs={{3,2},{7,6},{11,10},{15,14},{19,18},{23,22},{27,26},{31,30}} | collective-permute-start | bytes 2359304 | tf_op jit(solution)/shard_map/ppermute | solution.py:446
  51.6 14.2 %collective-permute-start.9 = (bf16[384,512]{1,0:T(8,128)(2,1)}, bf16[384,512]{1,0:T(8,128)(2,1)}, u32[]{:S(2)}, u32[]{:S(2)}) collective-permute-start(bf16[384,512]{1,0:T(8,128)(2,1)} %get-tuple-element.57.refs_1_), channel_id=1, source_target_pairs={{0,8},{4,12},{8,0},{12,4},{1,9},{5,13},{9,1},{13,5},{2,10},{6,14},... | collective-permute-start | bytes 1179656 | tf_op jit(solution)/shard_map/ppermute | solution.py:441
  62.6 10.9 %collective-permute-start.12 = (bf16[384,512]{1,0:T(8,128)(2,1)}, bf16[384,512]{1,0:T(8,128)(2,1)S(1)}, u32[]{:S(2)}, u32[]{:S(2)}) collective-permute-start(bf16[384,512]{1,0:T(8,128)(2,1)} %shard_map.86.refs_5_), channel_id=1, source_target_pairs={{0,8},{4,12},{8,0},{12,4},{1,9},{5,13},{9,1},{13,5},{2,10},{6,14},... | collective-permute-start | bytes 1179656 | tf_op jit(solution)/shard_map/ppermute | solution.py:489
  63.4 26.3 %collective-permute-start.14 = (bf16[512,1024]{1,0:T(8,128)(2,1)S(1)}, bf16[512,1024]{1,0:T(8,128)(2,1)S(1)}, u32[]{:S(2)}, u32[]{:S(2)}) collective-permute-start(bf16[512,1024]{1,0:T(8,128)(2,1)S(1)} %copy-done.1), channel_id=1, source_target_pairs={{0,16},{16,0},{1,17},{17,1},{2,18},{18,2},{3,19},{19,3},{4,20},{20... | collective-permute-start | bytes 3145736 | tf_op jit(solution)/shard_map/ppermute | solution.py:434
  65.8 8.6 %collective-permute-start.8 = (bf16[384,512]{1,0:T(8,128)(2,1)}, bf16[384,512]{1,0:T(8,128)(2,1)S(1)}, u32[]{:S(2)}, u32[]{:S(2)}) collective-permute-start(bf16[384,512]{1,0:T(8,128)(2,1)} %get-tuple-element.57.refs_1_), channel_id=1, source_target_pairs={{0,4},{4,0},{8,12},{12,8},{1,5},{5,1},{9,13},{13,9},{2,6},{6,2},{1... | collective-permute-start | bytes 1179656 | tf_op jit(solution)/shard_map/ppermute | solution.py:456
  73.5 64.8 %copy-start.8 = (bf16[384,512]{1,0:T(8,128)(2,1)}, bf16[384,512]{1,0:T(8,128)(2,1)S(1)}, u32[]{:S(2)}) copy-start(bf16[384,512]{1,0:T(8,128)(2,1)S(1)} %collective-permute-done.12.refs_7_) | copy-start | bytes 1179652
  73.5 2.5 %collective-permute-start.11 = (bf16[384,512]{1,0:T(8,128)(2,1)}, bf16[384,512]{1,0:T(8,128)(2,1)S(1)}, u32[]{:S(2)}, u32[]{:S(2)}) collective-permute-start(bf16[384,512]{1,0:T(8,128)(2,1)} %shard_map.86.refs_5_), channel_id=1, source_target_pairs={{0,4},{4,0},{8,12},{12,8},{1,5},{5,1},{9,13},{13,9},{2,6},{6,2},{1... | collective-permute-start | bytes 1179656 | tf_op jit(solution)/shard_map/ppermute | solution.py:456
  73.5 2.5 %collective-permute-start.10 = (bf16[384,512]{1,0:T(8,128)(2,1)}, bf16[384,512]{1,0:T(8,128)(2,1)S(1)}, u32[]{:S(2)}, u32[]{:S(2)}) collective-permute-start(bf16[384,512]{1,0:T(8,128)(2,1)} %collective-permute-done.9.refs_3_), channel_id=1, source_target_pairs={{0,4},{4,0},{8,12},{12,8},{1,5},{5,1},{9,13},{13,9},{2,6},{6,2},{1... | collective-permute-start | bytes 1179656 | tf_op jit(solution)/shard_map/ppermute | solution.py:457
  74.3 2.0 %collective-permute-start.13 = (bf16[384,512]{1,0:T(8,128)(2,1)S(1)}, bf16[384,512]{1,0:T(8,128)(2,1)S(1)}, u32[]{:S(2)}, u32[]{:S(2)}) collective-permute-start(bf16[384,512]{1,0:T(8,128)(2,1)S(1)} %collective-permute-done.12.refs_7_), channel_id=1, source_target_pairs={{0,4},{4,0},{8,12},{12,8},{1,5},{5,1},{9,13},{13,9},{2,6},{6,2},{1... | collective-permute-start | bytes 1179656 | tf_op jit(solution)/shard_map/ppermute | solution.py:457
  74.3 64.0 %copy-start.10 = (bf16[384,512]{1,0:T(8,128)(2,1)}, bf16[384,512]{1,0:T(8,128)(2,1)S(1)}, u32[]{:S(2)}) copy-start(bf16[384,512]{1,0:T(8,128)(2,1)S(1)} %collective-permute-done.8.refs_2_) | copy-start | bytes 1179652
  76.0 62.3 %copy-start.14 = (bf16[384,512]{1,0:T(8,128)(2,1)}, bf16[384,512]{1,0:T(8,128)(2,1)S(1)}, u32[]{:S(2)}) copy-start(bf16[384,512]{1,0:T(8,128)(2,1)S(1)} %collective-permute-done.10.refs_4_) | copy-start | bytes 1179652
  76.0 62.3 %copy-start.12 = (bf16[384,512]{1,0:T(8,128)(2,1)}, bf16[384,512]{1,0:T(8,128)(2,1)S(1)}, u32[]{:S(2)}) copy-start(bf16[384,512]{1,0:T(8,128)(2,1)S(1)} %collective-permute-done.11.refs_6_) | copy-start | bytes 1179652
  78.9 21.2 %collective-permute-start.15 = (bf16[768,512]{1,0:T(8,128)(2,1)S(1)}, bf16[768,512]{1,0:T(8,128)(2,1)S(1)}, u32[]{:S(2)}, u32[]{:S(2)}) collective-permute-start(bf16[768,512]{1,0:T(8,128)(2,1)S(1)} %get-tuple-element.62), channel_id=1, source_target_pairs={{0,1},{4,5},{8,9},{12,13},{16,17},{20,21},{24,25},{28,29}} | collective-permute-start | bytes 2359304 | tf_op jit(solution)/shard_map/ppermute | solution.py:445
  79.6 25.0 %collective-permute-start.16 = (bf16[768,512]{1,0:T(8,128)(2,1)S(1)}, bf16[768,512]{1,0:T(8,128)(2,1)S(1)}, u32[]{:S(2)}, u32[]{:S(2)}) collective-permute-start(bf16[768,512]{1,0:T(8,128)(2,1)S(1)} %get-tuple-element.63), channel_id=1, source_target_pairs={{3,2},{7,6},{11,10},{15,14},{19,18},{23,22},{27,26},{31,30}} | collective-permute-start | bytes 2359304 | tf_op jit(solution)/shard_map/ppermute | solution.py:446
  80.9 33.0 %collective-permute-start.17 = (bf16[512,1024]{1,0:T(8,128)(2,1)S(1)}, bf16[512,1024]{1,0:T(8,128)(2,1)S(1)}, u32[]{:S(2)}, u32[]{:S(2)}) collective-permute-start(bf16[512,1024]{1,0:T(8,128)(2,1)S(1)} %copy-done.3), channel_id=1, source_target_pairs={{0,16},{16,0},{1,17},{17,1},{2,18},{18,2},{3,19},{19,3},{4,20},{20... | collective-permute-start | bytes 3145736 | tf_op jit(solution)/shard_map/ppermute | solution.py:434
  94.1 22.4 %collective-permute-start.18 = (bf16[768,512]{1,0:T(8,128)(2,1)S(1)}, bf16[768,512]{1,0:T(8,128)(2,1)S(1)}, u32[]{:S(2)}, u32[]{:S(2)}) collective-permute-start(bf16[768,512]{1,0:T(8,128)(2,1)S(1)} %get-tuple-element.66), channel_id=1, source_target_pairs={{0,1},{1,2},{4,5},{5,6},{8,9},{9,10},{12,13},{13,14},{16,17},{17,1... | collective-permute-start | bytes 2359304 | tf_op jit(solution)/shard_map/ppermute | solution.py:445
  95.4 26.0 %collective-permute-start.19 = (bf16[768,512]{1,0:T(8,128)(2,1)S(1)}, bf16[768,512]{1,0:T(8,128)(2,1)S(1)}, u32[]{:S(2)}, u32[]{:S(2)}) collective-permute-start(bf16[768,512]{1,0:T(8,128)(2,1)S(1)} %get-tuple-element.67), channel_id=1, source_target_pairs={{2,1},{3,2},{6,5},{7,6},{10,9},{11,10},{14,13},{15,14},{18,17},{19... | collective-permute-start | bytes 2359304 | tf_op jit(solution)/shard_map/ppermute | solution.py:446
  108.0 25.7 %collective-permute-start.20 = (bf16[768,512]{1,0:T(8,128)(2,1)S(1)}, bf16[768,512]{1,0:T(8,128)(2,1)S(1)}, u32[]{:S(2)}, u32[]{:S(2)}) collective-permute-start(bf16[768,512]{1,0:T(8,128)(2,1)S(1)} %get-tuple-element.69), channel_id=1, source_target_pairs={{0,1},{1,2},{4,5},{5,6},{8,9},{9,10},{12,13},{13,14},{16,17},{17,1... | collective-permute-start | bytes 2359304 | tf_op jit(solution)/shard_map/ppermute | solution.py:445
  109.3 29.0 %collective-permute-start.21 = (bf16[768,512]{1,0:T(8,128)(2,1)S(1)}, bf16[768,512]{1,0:T(8,128)(2,1)S(1)}, u32[]{:S(2)}, u32[]{:S(2)}) collective-permute-start(bf16[768,512]{1,0:T(8,128)(2,1)S(1)} %get-tuple-element.70), channel_id=1, source_target_pairs={{2,1},{3,2},{6,5},{7,6},{10,9},{11,10},{14,13},{15,14},{18,17},{19... | collective-permute-start | bytes 2359304 | tf_op jit(solution)/shard_map/ppermute | solution.py:446
  113.9 37.1 %collective-permute-start.22 = (bf16[512,1024]{1,0:T(8,128)(2,1)S(1)}, bf16[512,1024]{1,0:T(8,128)(2,1)S(1)}, u32[]{:S(2)}, u32[]{:S(2)}) collective-permute-start(bf16[512,1024]{1,0:T(8,128)(2,1)S(1)} %copy-done.21), channel_id=1, source_target_pairs={{0,16},{16,0},{1,17},{17,1},{2,18},{18,2},{3,19},{19,3},{4,20},{20... | collective-permute-start | bytes 3145736 | tf_op jit(solution)/shard_map/ppermute | solution.py:434
  127.8 23.2 %collective-permute-start.23 = (bf16[768,512]{1,0:T(8,128)(2,1)S(1)}, bf16[768,512]{1,0:T(8,128)(2,1)S(1)}, u32[]{:S(2)}, u32[]{:S(2)}) collective-permute-start(bf16[768,512]{1,0:T(8,128)(2,1)S(1)} %get-tuple-element.73), channel_id=1, source_target_pairs={{0,1},{1,2},{2,3},{4,5},{5,6},{6,7},{8,9},{9,10},{10,11},{12,13},{... | collective-permute-start | bytes 2359304 | tf_op jit(solution)/shard_map/ppermute | solution.py:445
  129.8 25.4 %collective-permute-start.24 = (bf16[768,512]{1,0:T(8,128)(2,1)S(1)}, bf16[768,512]{1,0:T(8,128)(2,1)S(1)}, u32[]{:S(2)}, u32[]{:S(2)}) collective-permute-start(bf16[768,512]{1,0:T(8,128)(2,1)S(1)} %get-tuple-element.74), channel_id=1, source_target_pairs={{1,0},{2,1},{3,2},{5,4},{6,5},{7,6},{9,8},{10,9},{11,10},{13,12},{... | collective-permute-start | bytes 2359304 | tf_op jit(solution)/shard_map/ppermute | solution.py:446
  145.2 23.9 %collective-permute-start.25 = (bf16[768,512]{1,0:T(8,128)(2,1)}, bf16[768,512]{1,0:T(8,128)(2,1)}, u32[]{:S(2)}, u32[]{:S(2)}) collective-permute-start(bf16[768,512]{1,0:T(8,128)(2,1)} %get-tuple-element.76), channel_id=1, source_target_pairs={{0,1},{1,2},{2,3},{4,5},{5,6},{6,7},{8,9},{9,10},{10,11},{12,13},{... | collective-permute-start | bytes 2359304 | tf_op jit(solution)/shard_map/ppermute | solution.py:445
  147.1 24.4 %collective-permute-start.26 = (bf16[768,512]{1,0:T(8,128)(2,1)}, bf16[768,512]{1,0:T(8,128)(2,1)}, u32[]{:S(2)}, u32[]{:S(2)}) collective-permute-start(bf16[768,512]{1,0:T(8,128)(2,1)} %get-tuple-element.77), channel_id=1, source_target_pairs={{1,0},{2,1},{3,2},{5,4},{6,5},{7,6},{9,8},{10,9},{11,10},{13,12},{... | collective-permute-start | bytes 2359304 | tf_op jit(solution)/shard_map/ppermute | solution.py:446
  (24 other events, 272.6 us)

commit v3 on v2

--- a/solution.py
+++ b/solution.py
@@ -99,14 +99,6 @@
     moves(cells_lane[...], fill.shape[0], fill, spare, on_rim)
 
 
-def pick_kernel(where, table, whole, out, sem):
-    rows = out.shape[0]
-    first = pl.multiple_of(table[where[2], 0] * rows, rows)
-    copy = pltpu.make_async_copy(whole.at[pl.ds(first, rows), :], out, sem)
-    copy.start()
-    copy.wait()
-
-
 def read_kernel(rows_of, cols_of, count, shards, *refs):
     refs = list(refs)
     dev, before, after, courant, cells_lane = (refs.pop(0) for _ in range(5))
@@ -120,7 +112,7 @@
         stage, in_sem, out_sem = refs
         rows = stage.shape[1]
         for j in range(shards):
-            first = pl.multiple_of(table[where[2], j + 1] * rows, rows)
+            first = pl.multiple_of(table[where[2], j] * rows, rows)
             fetches.append(
                 pltpu.make_async_copy(whole.at[pl.ds(first, rows), :], stage.at[j], in_sem.at[j])
             )
@@ -210,41 +202,32 @@
     out[...] = jnp.where(used, emitted, extra[...].astype(jnp.float32)).astype(out.dtype)
 
 
-def ends_kernel(fill, *refs):
-    parts, ends = refs[:-1], refs[-1]
-    total, first = None, 0
-    for part in parts:
-        rows = slice(first, first + part.shape[0])
-        first += part.shape[0]
-        moved = lax.dot_general(
-            fill[rows, :], part[...], (((0,), (0,)), ((), ())), preferred_element_type=jnp.float32
-        )
-        total = moved if total is None else total + moved
-    ends[...] = total
-
-
-def merge_kernel(fill, spare, place, on_rim, ends, total, from_left, from_right, *refs):
-    parts, out = refs[:-1], refs[-1]
-    head = on_rim.shape[0]
+def base_kernel(fill, on_rim, part, base):
+    kept = part.shape[0]
+    base[:kept, :] = jnp.where(on_rim[...] > 0, 0.0, part[...].astype(jnp.float32)).astype(base.dtype)
+    moved = lax.dot_general(
+        fill[...], part[...], (((0,), (0,)), ((), ())), preferred_element_type=jnp.float32
+    )
+    base[kept:, :] = moved.astype(base.dtype)
+
+
+def merge_kernel(fill, spare, place, on_rim, base, total, from_left, from_right, out):
     slots = spare.shape[0]
+    kept = base.shape[0] - slots
     total = total[...] + from_left[...].astype(jnp.float32) + from_right[...].astype(jnp.float32)
     total = total.astype(jnp.bfloat16)
-    kept = total.shape[0] - slots
-    last = total[kept:, :]
-    parts = [part[...] for part in parts] + [total[:kept, :]]
+    more = total.shape[0] - slots
+    part, last = total[:more, :], total[more:, :]
+    head = kept + more
     tn = (((0,), (0,)), ((), ()))
-    back = lax.dot_general(spare[...], last, tn, preferred_element_type=jnp.float32)
-    back = back + jnp.dot(place[head:, :], last, preferred_element_type=jnp.float32)
-    back = back + lax.dot_general(
-        fill[head - kept :, :], parts[-1], tn, preferred_element_type=jnp.float32
-    )
-    out[head:, :] = (back + ends[...]).astype(out.dtype)
-    first = 0
-    for part in parts:
-        rows = slice(first, first + part.shape[0])
-        first += part.shape[0]
-        moved = jnp.dot(place[rows, :], last, preferred_element_type=jnp.float32)
-        out[rows, :] = jnp.where(on_rim[rows, :] > 0, moved, part.astype(jnp.float32)).astype(out.dtype)
+    moved = jnp.dot(place[:kept, :], last, preferred_element_type=jnp.float32)
+    out[:kept, :] = (base[:kept, :].astype(jnp.float32) + moved).astype(out.dtype)
+    moved = jnp.dot(place[kept:head, :], last, preferred_element_type=jnp.float32)
+    out[kept:head, :] = jnp.where(on_rim[...] > 0, moved, part.astype(jnp.float32)).astype(out.dtype)
+    moved = jnp.dot(place[head:, :], last, preferred_element_type=jnp.float32)
+    moved = moved + lax.dot_general(spare[...], last, tn, preferred_element_type=jnp.float32)
+    moved = moved + lax.dot_general(fill[...], part, tn, preferred_element_type=jnp.float32)
+    out[head:, :] = (base[kept:, :].astype(jnp.float32) + moved).astype(out.dtype)
 
 
 def hop_kernel(t, size, wide, slots, groups, has_recv, *refs):
@@ -368,10 +351,16 @@
     params = pltpu.CompilerParams(vmem_limit_bytes=LIMIT)
     where = jnp.stack([s, r, c]).astype(jnp.int32)
 
-    up = [(i, i + 1) for i in range(n_space - 1)]
-    down = [(j, i) for i, j in up]
-    before_layer = lax.ppermute(deviation[-1:], "space", up)
-    after_layer = lax.ppermute(deviation[:1], "space", down)
+    if n_space == 2:
+        edge = jnp.where(s == 0, deviation[-1:], deviation[:1])
+        edge = lax.ppermute(edge, "space", [(0, 1), (1, 0)])
+        none = jnp.zeros_like(edge)
+        before_layer, after_layer = jnp.where(s == 1, edge, none), jnp.where(s == 0, edge, none)
+    else:
+        up = [(i, i + 1) for i in range(n_space - 1)]
+        down = [(j, i) for i, j in up]
+        before_layer = lax.ppermute(deviation[-1:], "space", up)
+        after_layer = lax.ppermute(deviation[:1], "space", down)
 
     def after(value, *first):
         return lax.optimization_barrier((value, first))[0]
@@ -386,20 +375,9 @@
     wide = n_space != 2
     rows = collide.shape[0] // n_col
     own = lax.all_gather(collide, "space", axis=1, tiled=True) if wide else None
-    shards = 0 if wide else n_col - 1
+    shards = 0 if wide else n_col
     swap = [(0, 1), (1, 0)]
-    held, order, first = [], jnp.asarray(line_steps(n_col)), ()
-    if not wide:
-        first = pl.pallas_call(
-            pick_kernel,
-            out_shape=shape(rows, collide.shape[1]),
-            in_specs=[smem, smem, hbm],
-            out_specs=vmem,
-            scratch_shapes=[pltpu.SemaphoreType.DMA],
-            compiler_params=params,
-            cost_estimate=takes(2),
-        )(where, order, collide)
-        held.append((first, lax.ppermute(after(first, before_layer, after_layer), "space", swap)))
+    held, order = [], jnp.asarray(line_steps(n_col))
     payload, extra, *mine = pl.pallas_call(
         functools.partial(read_kernel, n_row, n_col, count, shards),
         out_shape=[shape(groups, piece + TAIL, slot_count), shape(slot_count, block_len)]
@@ -426,7 +404,7 @@
         before_layer,
         after_layer,
         courant,
-        after(lane_cells, first),
+        lane_cells,
         *([] if wide else [where, order, collide]),
     )
     mine, parts = mine[:count], mine[count:]
@@ -472,9 +450,9 @@
         compiler_params=params,
         cost_estimate=takes(4),
     )(after(lane_cells, extra), own_table)
-    far[0] = after(far[0], mirror)
+    far[0] = after(far[0], mirror, *[other for _, other in held[:1]])
     chunks = [[gather(0)]]
-    done = step(1, 0)
+    done = step(1, 0, arrived)
     state[0] = send(1, done)
     mine.append(
         pl.pallas_call(
@@ -484,7 +462,7 @@
             out_specs=vmem,
             compiler_params=params,
             cost_estimate=takes(4),
-        )(specularity, after(arrived, *done), mirror, hole_wall[None, :], lane_cells, extra)
+        )(specularity, after(arrived, far[1], *done), mirror, hole_wall[None, :], lane_cells, extra)
     )
     far.append(lax.ppermute(mine[count], "mrow", flip[1]))
     chunks.append([gather(n) for n in range(1, count + 1)])
@@ -501,22 +479,28 @@
             else:
                 state[n] = send(t, done)
     total = hop(n_col, n_col, after(where, *done), chunks[1], own, held, None)[0]
-    ends = pl.pallas_call(
-        ends_kernel,
-        out_shape=jax.ShapeDtypeStruct((slot_count, rows), jnp.float32),
-        in_specs=[vmem] * (1 + len(outs)),
-        out_specs=vmem,
+    base = pl.pallas_call(
+        base_kernel,
+        out_shape=shape(sizes[0] + slot_count, rows),
+        grid=(1,),
+        in_specs=[
+            pl.BlockSpec((sizes[0], slot_count), lambda i: (0, 0)),
+            pl.BlockSpec((sizes[0], 1), lambda i: (0, 0)),
+            pl.BlockSpec((sizes[0], rows), lambda i: (0, 0)),
+        ],
+        out_specs=pl.BlockSpec((sizes[0] + slot_count, rows), lambda i: (0, 0)),
         compiler_params=params,
         cost_estimate=takes(2),
-    )(fill, *outs)
+    )(fill, on_rim, *outs)
+    near = pl.BlockSpec(memory_space=pltpu.VMEM)
     out = pl.pallas_call(
         merge_kernel,
         out_shape=shape(cell_count, rows),
-        in_specs=[vmem] * (8 + len(outs)),
+        in_specs=[near] * 8,
         out_specs=vmem,
-        compiler_params=params,
+        compiler_params=pltpu.CompilerParams(vmem_limit_bytes=HOP_LIMIT),
         cost_estimate=takes(4),
-    )(fill, spare, place, on_rim, ends, total, *state[1], *outs)
+    )(fill[sizes[0] :], spare, place, on_rim[sizes[0] :], base, total, *state[1])
     return out.reshape(width_x, width_y, rows)
 
 

time: 179 us -> 168 us (0.939)
  starting transfers between devices: 52.4 us -> 41.9 us
  Pallas kernels: 60.9 us -> 56.1 us
  waiting for transfers between devices: 54.1 us -> 56.6 us
    all_to_all x1, waiting for transfers between devices: 5.95 us -> 0.01 us  [on_device(): lax.all_to_all(payload, ('mrow', 'mcol'), split_axis=0, concat_axis=0, ti...]
    ppermute x3 -> x1, starting transfers between devices: 7.32 us -> 1.49 us  [on_device(): edge = lax.ppermute(edge, 'space', [(0, 1), (1, 0)])]
    ppermute x3 -> x4, starting transfers between devices: 7.23 us -> 3.6 us  [on_device(): held.append((part, lax.ppermute(part, 'space', swap)))]
    ppermute x2, waiting for transfers between devices: 11 us -> 14.5 us  [on_device(): far.append(lax.ppermute(value, 'mrow', flip[1]))]
    pallas_call x2 -> x1, Pallas kernels: 5.97 us -> 3.11 us  [on_device(): pl.pallas_call(base_kernel, out_shape=shape(sizes[0] + slot_count, rows),...]
    ppermute x6, waiting for transfers between devices: 20.9 us -> 23.3 us  [send(): lax.ppermute(value[1], 'mcol', left[n_col - 1 - t:])]
    pallas_call x1, Pallas kernels: 5.77 us -> 3.76 us  [on_device(): pl.pallas_call(merge_kernel, out_shape=shape(cell_count, rows), in_specs=...]
    ppermute x1, waiting for transfers between devices: 7.73 us -> 9.71 us  [on_device(): far.append(lax.ppermute(mine[count], 'mrow', flip[1]))]
  transfers between devices with their start and end apart: 28 -> 27, of which waited for: 13 -> 13; matrix products, arithmetic and copies ran while one was open for 2% -> 3% of each run, Pallas kernels for 27% -> 27%
where the time goes in v3:
time: 168 us; the launch traced here: 167 us
  waiting for transfers between devices  56.6 us (34%)
  Pallas kernels  56.1 us (33%)
  starting transfers between devices  41.9 us (25%)
  local copies, waits for them, and re-layouts  9.71 us (6%)
  other arithmetic  2.07 us (1%)
    pallas_call x8, Pallas kernels, hop(): pl.pallas_call(functools.partial(hop_kernel, t, size, wide, slots, len(bl...  32.7 us
    ppermute x6, waiting for transfers between devices, send(): lax.ppermute(value[1], 'mcol', left[n_col - 1 - t:])  23.3 us
    ppermute x6, starting transfers between devices, send(): lax.ppermute(value[1], 'mcol', left[n_col - 1 - t:])  19.6 us
    ppermute x2, waiting for transfers between devices, on_device(): far.append(lax.ppermute(value, 'mrow', flip[1]))  14.5 us
    ppermute x1, waiting for transfers between devices, on_device(): far.append(lax.ppermute(mine[count], 'mrow', flip[1]))  9.71 us
    ppermute x6, starting transfers between devices, send(): lax.ppermute(value[0], 'mcol', right[:t])  8.7 us
    pallas_call x1, Pallas kernels, on_device(): pl.pallas_call(functools.partial(read_kernel, n_row, n_col, count, shards...  8.12 us
    all_to_all x1, starting transfers between devices, on_device(): lax.all_to_all(payload, ('mrow', 'mcol'), split_axis=0, concat_axis=0, ti...  6.19 us
  transfers between devices with their start and end apart: 27, of which 13 were waited for; matrix products, arithmetic and copies ran while one was open for 3% of the time, Pallas kernels for 27%

profile of v3, /device:TPU:20, one launch (start us, length us, event | category | flops | bytes accessed | tf_op | source)
XLA Modules:
  0.0 166.8 jit_solution(2981374506600340888)
XLA Ops:
  5.6 8.1 %shard_map.82 = (bf16[16,48,384]{2,1,0:T(8,128)(2,1)}, bf16[384,512]{1,0:T(8,128)(2,1)}, bf16[768,512]{1,0:T(8,128)(2,1)}, bf16[384,512]{1,0:T(8,128)(2,1)}, bf1...) custom-call(bf16[32,48,512]{2,1,0:T(8,128)(2,1)} %refs_0_.1, ...), custom_call_target="tpu_custom_call" | custom-call | flops 3500000000 | tf_op jit(solution)/shard_map/pallas_call | solution.py:381
  13.7 1.6 collective-permute-start.3
  15.8 6.2 %all-to-all-start = ((bf16[16,48,384]{2,1,0:T(8,128)(2,1)}), bf16[16,48,384]{2,1,0:T(8,128)(2,1)}, u32[]{:S(2)}, u32[]{:S(2)}) async-start(bf16[16,48,384]{2,1,0:T(8,128)(2,1)} %get-tuple-element.49), calls=%async_computation | async-start | bytes 1179648 | tf_op jit(solution)/shard_map/all_to_all | solution.py:420
  22.7 4.7 %shard_map.83 = (bf16[4,512,512]{2,1,0:T(8,128)(2,1)}, bf16[1536,384]{1,0:T(8,128)(2,1)}, bf16[1152,384]{1,0:T(8,128)(2,1)}, bf16[384,384]{1,0:T(8,128)(2,1)}, f32[1152,1]{1,0:T(8,128)}) custom-call(s32[1,384]{1,0:T(1,128)} %broadcast_in_dim.9.refs_4_.cells_lane, s32[4,512]{1,0:T(4,128)} %constant_dynamic-slice_fusion.table), custom_call_target="tpu_custom_call" | custom-call | flops 2000000000 | tf_op jit(solution)/shard_map/pallas_call | solution.py:439
  27.5 11.5 %collective-permute-done.2.refs_3_ = bf16[768,512]{1,0:T(8,128)(2,1)} collective-permute-done((bf16[768,512]{1,0:T(8,128)(2,1)}, bf16[768,512]{1,0:T(8,128)(2,1)}, u32[]{:S(2)}, u32[]{:S(2)}) %collective-permute-start.2) | collective-permute-done | bytes 786464 | tf_op jit(solution)/shard_map/ppermute | solution.py:419
  39.6 2.0 %collective-permute-done.4.refs_4_ = bf16[768,512]{1,0:T(8,128)(2,1)} collective-permute-done((bf16[768,512]{1,0:T(8,128)(2,1)}, bf16[768,512]{1,0:T(8,128)(2,1)}, u32[]{:S(2)}, u32[]{:S(2)}) %collective-permute-start.4) | collective-permute-done | bytes 786464 | tf_op jit(solution)/shard_map/ppermute | solution.py:435
  41.6 2.8 %shard_map.84 = (bf16[768,512]{1,0:T(8,128)(2,1)}, bf16[768,512]{1,0:T(8,128)(2,1)}) custom-call(s32[3]{0:T(128)S(1)} %copy-done.21, bf16[768,512]{1,0:T(8,128)(2,1)S(1)} %copy-done.4, bf16[768,512]{1,0:T(8,128)(2,1)} %collective-permute-done.1.refs_2_, bf16[768,512]{1,0:T(8,128)(2,1)} %collective-permute-done.2.refs_3_, ...), custom_call_target="tpu_custom_call" | custom-call | flops 2280000000 | tf_op jit(solution)/shard_map/pallas_call | solution.py:325
  44.4 1.6 collective-permute-start.5
  47.8 3.0 %collective-permute-done.8.refs_3_ = bf16[384,512]{1,0:T(8,128)(2,1)} collective-permute-done((bf16[384,512]{1,0:T(8,128)(2,1)}, bf16[384,512]{1,0:T(8,128)(2,1)}, u32[]{:S(2)}, u32[]{:S(2)}) %collective-permute-start.8) | collective-permute-done | bytes 393248 | tf_op jit(solution)/shard_map/ppermute | solution.py:419
  50.8 3.7 %shard_map.85.refs_5_ = bf16[384,512]{1,0:T(8,128)(2,1)} custom-call(f32[4]{0:T(128)} %specularity.1, bf16[16,48,384]{2,1,0:T(8,128)(2,1)} %all-to-all-done.arrived, bf16[4,512,512]{2,1,0:T(8,128)(2,1)} %get-tuple-element.52.mirror, s32[1,384]{1,0:T(1,128)} %broadcast_in_dim.11.wall, s32[1,384]{1,0:T(1,128)} %broadcast_in_dim.9.refs_4_.cells_lane, ...), custom_call_target="tpu_custom_call" | custom-call | flops 2000000000 | tf_op jit(solution)/shard_map/pallas_call | solution.py:458
  55.7 9.7 %collective-permute-done.11.refs_7_ = bf16[384,512]{1,0:T(8,128)(2,1)S(1)} collective-permute-done((bf16[384,512]{1,0:T(8,128)(2,1)}, bf16[384,512]{1,0:T(8,128)(2,1)S(1)}, u32[]{:S(2)}, u32[]{:S(2)}) %collective-permute-start.11) | collective-permute-done | bytes 393248 | tf_op jit(solution)/shard_map/ppermute | solution.py:467
  65.9 3.2 %collective-permute-done.6.refs_10_ = bf16[768,512]{1,0:T(8,128)(2,1)} collective-permute-done((bf16[768,512]{1,0:T(8,128)(2,1)}, bf16[768,512]{1,0:T(8,128)(2,1)}, u32[]{:S(2)}, u32[]{:S(2)}) %collective-permute-start.6) | collective-permute-done | bytes 786464 | tf_op jit(solution)/shard_map/ppermute | solution.py:424
  69.2 1.7 %collective-permute-done.12.refs_8_ = bf16[384,512]{1,0:T(8,128)(2,1)S(1)} collective-permute-done((bf16[384,512]{1,0:T(8,128)(2,1)S(1)}, bf16[384,512]{1,0:T(8,128)(2,1)S(1)}, u32[]{:S(2)}, u32[]{:S(2)}) %collective-permute-start.12) | collective-permute-done | bytes 393248 | tf_op jit(solution)/shard_map/ppermute | solution.py:435
  76.1 4.6 %collective-permute-done.13.refs_8_.refs_12_.refs_6_.refs_10_ = bf16[512,1024]{1,0:T(8,128)(2,1)S(1)} collective-permute-done((bf16[512,1024]{1,0:T(8,128)(2,1)S(1)}, bf16[512,1024]{1,0:T(8,128)(2,1)S(1)}, u32[]{:S(2)}, u32[]{:S(2)}) %collective-permute-start.13) | collective-permute-done | bytes 1048608 | tf_op jit(solution)/shard_map/ppermute | solution.py:412
  80.7 4.4 %shard_map.87 = (bf16[768,512]{1,0:T(8,128)(2,1)S(1)}, bf16[768,512]{1,0:T(8,128)(2,1)S(1)}) custom-call(s32[3]{0:T(128)S(1)} %copy-done.21, bf16[768,512]{1,0:T(8,128)(2,1)S(1)} %copy-done.5, bf16[768,512]{1,0:T(8,128)(2,1)} %collective-permute-done.1.refs_2_, bf16[768,512]{1,0:T(8,128)(2,1)} %collective-permute-done.2.refs_3_, ...), custom_call_target="tpu_custom_call" | custom-call | flops 2280000000 | tf_op jit(solution)/shard_map/pallas_call | solution.py:325
  86.4 4.7 %collective-permute-start.18 = (bf16[768,512]{1,0:T(8,128)(2,1)S(1)}, bf16[768,512]{1,0:T(8,128)(2,1)S(1)}, u32[]{:S(2)}, u32[]{:S(2)}) collective-permute-start(bf16[768,512]{1,0:T(8,128)(2,1)S(1)} %get-tuple-element.67), channel_id=1, source_target_pairs={{2,1},{3,2},{6,5},{7,6},{10,9},{11,10},{14,13},{15,14},{18,17},{19... | collective-permute-start | bytes 2359304 | tf_op jit(solution)/shard_map/ppermute | solution.py:424
  91.1 5.3 %collective-permute-done.15.refs_14_ = bf16[768,512]{1,0:T(8,128)(2,1)S(1)} collective-permute-done((bf16[768,512]{1,0:T(8,128)(2,1)S(1)}, bf16[768,512]{1,0:T(8,128)(2,1)S(1)}, u32[]{:S(2)}, u32[]{:S(2)}) %collective-permute-start.15) | collective-permute-done | bytes 786464 | tf_op jit(solution)/shard_map/ppermute | solution.py:424
  96.4 3.4 %shard_map.88 = (bf16[768,512]{1,0:T(8,128)(2,1)S(1)}, bf16[768,512]{1,0:T(8,128)(2,1)S(1)}) custom-call(s32[3]{0:T(128)S(1)} %copy-done.21, bf16[384,512]{1,0:T(8,128)(2,1)} %get-tuple-element.58.refs_1_, bf16[384,512]{1,0:T(8,128)(2,1)S(1)} %collective-permute-done.7.refs_2_, bf16[384,512]{1,0:T(8,128)(2,1)} %collective-permute-done.8.refs_3_, ...), custom_call_target="tpu_custom_call" | custom-call | flops 2280000000 | tf_op jit(solution)/shard_map/pallas_call | solution.py:325
  101.1 4.6 %collective-permute-start.20 = (bf16[768,512]{1,0:T(8,128)(2,1)S(1)}, bf16[768,512]{1,0:T(8,128)(2,1)S(1)}, u32[]{:S(2)}, u32[]{:S(2)}) collective-permute-start(bf16[768,512]{1,0:T(8,128)(2,1)S(1)} %get-tuple-element.70), channel_id=1, source_target_pairs={{2,1},{3,2},{6,5},{7,6},{10,9},{11,10},{14,13},{15,14},{18,17},{19... | collective-permute-start | bytes 2359304 | tf_op jit(solution)/shard_map/ppermute | solution.py:424
  106.4 6.8 %collective-permute-done.18.refs_10_ = bf16[768,512]{1,0:T(8,128)(2,1)S(1)} collective-permute-done((bf16[768,512]{1,0:T(8,128)(2,1)S(1)}, bf16[768,512]{1,0:T(8,128)(2,1)S(1)}, u32[]{:S(2)}, u32[]{:S(2)}) %collective-permute-start.18) | collective-permute-done | bytes 786464 | tf_op jit(solution)/shard_map/ppermute | solution.py:424
  113.2 6.4 %shard_map.89 = (bf16[768,512]{1,0:T(8,128)(2,1)S(1)}, bf16[768,512]{1,0:T(8,128)(2,1)S(1)}) custom-call(s32[3]{0:T(128)S(1)} %copy-done.21, bf16[768,512]{1,0:T(8,128)(2,1)S(1)} %copy-done.5, bf16[768,512]{1,0:T(8,128)(2,1)} %collective-permute-done.1.refs_2_, bf16[768,512]{1,0:T(8,128)(2,1)} %collective-permute-done.2.refs_3_, ...), custom_call_target="tpu_custom_call" | custom-call | flops 2280000000 | tf_op jit(solution)/shard_map/pallas_call | solution.py:325
  119.6 1.9 %collective-permute-start.22 = (bf16[768,512]{1,0:T(8,128)(2,1)S(1)}, bf16[768,512]{1,0:T(8,128)(2,1)S(1)}, u32[]{:S(2)}, u32[]{:S(2)}) collective-permute-start(bf16[768,512]{1,0:T(8,128)(2,1)S(1)} %get-tuple-element.73), channel_id=1, source_target_pairs={{0,1},{1,2},{2,3},{4,5},{5,6},{6,7},{8,9},{9,10},{10,11},{12,13},{... | collective-permute-start | bytes 2359304 | tf_op jit(solution)/shard_map/ppermute | solution.py:423
  121.5 3.9 %collective-permute-start.23 = (bf16[768,512]{1,0:T(8,128)(2,1)S(1)}, bf16[768,512]{1,0:T(8,128)(2,1)S(1)}, u32[]{:S(2)}, u32[]{:S(2)}) collective-permute-start(bf16[768,512]{1,0:T(8,128)(2,1)S(1)} %get-tuple-element.74), channel_id=1, source_target_pairs={{1,0},{2,1},{3,2},{5,4},{6,5},{7,6},{9,8},{10,9},{11,10},{13,12},{... | collective-permute-start | bytes 2359304 | tf_op jit(solution)/shard_map/ppermute | solution.py:424
  125.5 4.6 %collective-permute-done.20.refs_14_ = bf16[768,512]{1,0:T(8,128)(2,1)S(1)} collective-permute-done((bf16[768,512]{1,0:T(8,128)(2,1)S(1)}, bf16[768,512]{1,0:T(8,128)(2,1)S(1)}, u32[]{:S(2)}, u32[]{:S(2)}) %collective-permute-start.20) | collective-permute-done | bytes 786464 | tf_op jit(solution)/shard_map/ppermute | solution.py:424
  130.1 6.9 %shard_map.90 = (bf16[768,512]{1,0:T(8,128)(2,1)}, bf16[768,512]{1,0:T(8,128)(2,1)}) custom-call(s32[3]{0:T(128)S(1)} %copy-done.21, bf16[384,512]{1,0:T(8,128)(2,1)} %get-tuple-element.58.refs_1_, bf16[384,512]{1,0:T(8,128)(2,1)S(1)} %collective-permute-done.7.refs_2_, bf16[384,512]{1,0:T(8,128)(2,1)} %collective-permute-done.8.refs_3_, ...), custom_call_target="tpu_custom_call" | custom-call | flops 2280000000 | tf_op jit(solution)/shard_map/pallas_call | solution.py:325
  137.0 1.9 %collective-permute-start.24 = (bf16[768,512]{1,0:T(8,128)(2,1)}, bf16[768,512]{1,0:T(8,128)(2,1)S(1)}, u32[]{:S(2)}, u32[]{:S(2)}) collective-permute-start(bf16[768,512]{1,0:T(8,128)(2,1)} %get-tuple-element.76), channel_id=1, source_target_pairs={{0,1},{1,2},{2,3},{4,5},{5,6},{6,7},{8,9},{9,10},{10,11},{12,13},{... | collective-permute-start | bytes 2359304 | tf_op jit(solution)/shard_map/ppermute | solution.py:423
  138.9 3.9 %collective-permute-start.25 = (bf16[768,512]{1,0:T(8,128)(2,1)}, bf16[768,512]{1,0:T(8,128)(2,1)}, u32[]{:S(2)}, u32[]{:S(2)}) collective-permute-start(bf16[768,512]{1,0:T(8,128)(2,1)} %get-tuple-element.77), channel_id=1, source_target_pairs={{1,0},{2,1},{3,2},{5,4},{6,5},{7,6},{9,8},{10,9},{11,10},{13,12},{... | collective-permute-start | bytes 2359304 | tf_op jit(solution)/shard_map/ppermute | solution.py:424
  144.8 2.1 %collective-permute-done.23.refs_8_ = bf16[768,512]{1,0:T(8,128)(2,1)S(1)} collective-permute-done((bf16[768,512]{1,0:T(8,128)(2,1)S(1)}, bf16[768,512]{1,0:T(8,128)(2,1)S(1)}, u32[]{:S(2)}, u32[]{:S(2)}) %collective-permute-start.23) | collective-permute-done | bytes 786464 | tf_op jit(solution)/shard_map/ppermute | solution.py:424
  146.9 3.8 %shard_map.91.part = bf16[768,512]{1,0:T(8,128)(2,1)S(1)} custom-call(s32[3]{0:T(128)S(1)} %copy-done.21, bf16[768,512]{1,0:T(8,128)(2,1)S(1)} %copy-done.5, bf16[768,512]{1,0:T(8,128)(2,1)} %collective-permute-done.1.refs_2_, bf16[768,512]{1,0:T(8,128)(2,1)} %collective-permute-done.2.refs_3_, bf16[768,512]{1,0:T(8,128)(2,1)} %collective-permute-done.4.refs_4_, ...), custom_call_target="tpu_custom_call" | custom-call | flops 2280000000 | tf_op jit(solution)/shard_map/pallas_call | solution.py:325
  152.6 3.1 %shard_map.92.base = bf16[1152,512]{1,0:T(8,128)(2,1)} custom-call(bf16[1152,384]{1,0:T(8,128)(2,1)} %get-tuple-element.45.fill, f32[1152,1]{1,0:T(8,128)} %get-tuple-element.48.on_rim, bf16[768,512]{1,0:T(8,128)(2,1)} %copy-done.26), custom_call_target="tpu_custom_call" | custom-call | flops 1000000000 | tf_op jit(solution)/shard_map/pallas_call | solution.py:482
  158.2 3.5 %shard_map.93.total = f32[768,512]{1,0:T(8,128)S(1)} custom-call(s32[3]{0:T(128)S(1)} %copy-done.21, bf16[384,512]{1,0:T(8,128)(2,1)} %get-tuple-element.58.refs_1_, bf16[384,512]{1,0:T(8,128)(2,1)S(1)} %copy-done.11, bf16[384,512]{1,0:T(8,128)(2,1)} %collective-permute-done.8.refs_3_, bf16[384,512]{1,0:T(8,128)(2,1)S(1)} %copy-done.15, ...), custom_call_target="tpu_custom_call" | custom-call | flops 2280000000 | tf_op jit(solution)/shard_map/pallas_call | solution.py:325
  163.1 3.8 %shard_map.94 = bf16[1536,512]{1,0:T(8,128)(2,1)} custom-call(bf16[384,384]{1,0:T(8,128)(2,1)S(1)} %slice.14.fill, bf16[384,384]{1,0:T(8,128)(2,1)S(1)} %copy-done.20, bf16[1536,384]{1,0:T(8,128)(2,1)S(1)} %copy-done.18, f32[384,1]{1,0:T(8,128)S(1)} %slice.15.on_rim, bf16[1152,512]{1,0:T(8,128)(2,1)S(1)} %copy-done.19, f32[768,512]{1,0:T(8,128)S(1)} %shard_map.93.total, ...), custom_call_target="tpu_custom_call" | custom-call | flops 2000000000 | tf_op jit(solution)/shard_map/pallas_call | solution.py:496
  (99 shorter events, 27.0 us)
Async XLA Ops:
  0.9 4.1 %collective-permute-start = (bf16[1,48,512]{2,1,0:T(8,128)(2,1)S(1)}, bf16[1,48,512]{2,1,0:T(8,128)(2,1)S(1)}, u32[]{:S(2)}, u32[]{:S(2)}) collective-permute-start(bf16[1,48,512]{2,1,0:T(8,128)(2,1)S(1)} %slice_select_fusion), channel_id=1, source_target_pairs={{0,16},{16,0},{1,17},{17,1},{2,18},{18,2},{3,19},{19,3},{4,20},{20... | collective-permute-start | bytes 147464 | tf_op jit(solution)/shard_map/ppermute | solution.py:356
  13.7 25.3 %collective-permute-start.3 = (bf16[512,1024]{1,0:T(8,128)(2,1)}, bf16[512,1024]{1,0:T(8,128)(2,1)S(1)}, u32[]{:S(2)}, u32[]{:S(2)}) collective-permute-start(bf16[512,1024]{1,0:T(8,128)(2,1)} %get-tuple-element.53.refs_5_.refs_9_), channel_id=1, source_target_pairs={{0,16},{16,0},{1,17},{17,1},{2,18},{18,2},{3,19},{19,3},{4,20},{20... | collective-permute-start | bytes 3145736 | tf_op jit(solution)/shard_map/ppermute | solution.py:412
  15.3 23.7 %collective-permute-start.2 = (bf16[768,512]{1,0:T(8,128)(2,1)}, bf16[768,512]{1,0:T(8,128)(2,1)}, u32[]{:S(2)}, u32[]{:S(2)}) collective-permute-start(bf16[768,512]{1,0:T(8,128)(2,1)} %get-tuple-element.51.refs_1_), channel_id=1, source_target_pairs={{0,8},{4,12},{8,0},{12,4},{1,9},{5,13},{9,1},{13,5},{2,10},{6,14},... | collective-permute-start | bytes 2359304 | tf_op jit(solution)/shard_map/ppermute | solution.py:419
  15.8 23.8 %all-to-all-start = ((bf16[16,48,384]{2,1,0:T(8,128)(2,1)}), bf16[16,48,384]{2,1,0:T(8,128)(2,1)}, u32[]{:S(2)}, u32[]{:S(2)}) async-start(bf16[16,48,384]{2,1,0:T(8,128)(2,1)} %get-tuple-element.49), calls=%async_computation | async-start | bytes 1179648 | tf_op jit(solution)/shard_map/all_to_all | solution.py:420
  22.6 17.0 %collective-permute-start.1 = (bf16[768,512]{1,0:T(8,128)(2,1)}, bf16[768,512]{1,0:T(8,128)(2,1)}, u32[]{:S(2)}, u32[]{:S(2)}) collective-permute-start(bf16[768,512]{1,0:T(8,128)(2,1)} %get-tuple-element.51.refs_1_), channel_id=1, source_target_pairs={{0,4},{4,0},{8,12},{12,8},{1,5},{5,1},{9,13},{13,9},{2,6},{6,2},{1... | collective-permute-start | bytes 2359304 | tf_op jit(solution)/shard_map/ppermute | solution.py:434
  39.0 2.6 %collective-permute-start.4 = (bf16[768,512]{1,0:T(8,128)(2,1)}, bf16[768,512]{1,0:T(8,128)(2,1)}, u32[]{:S(2)}, u32[]{:S(2)}) collective-permute-start(bf16[768,512]{1,0:T(8,128)(2,1)} %collective-permute-done.2.refs_3_), channel_id=1, source_target_pairs={{0,4},{4,0},{8,12},{12,8},{1,5},{5,1},{9,13},{13,9},{2,6},{6,2},{1... | collective-permute-start | bytes 2359304 | tf_op jit(solution)/shard_map/ppermute | solution.py:435
  39.0 11.8 %collective-permute-start.8 = (bf16[384,512]{1,0:T(8,128)(2,1)}, bf16[384,512]{1,0:T(8,128)(2,1)}, u32[]{:S(2)}, u32[]{:S(2)}) collective-permute-start(bf16[384,512]{1,0:T(8,128)(2,1)} %get-tuple-element.58.refs_1_), channel_id=1, source_target_pairs={{0,8},{4,12},{8,0},{12,4},{1,9},{5,13},{9,1},{13,5},{2,10},{6,14},... | collective-permute-start | bytes 1179656 | tf_op jit(solution)/shard_map/ppermute | solution.py:419
  44.4 21.0 %collective-permute-start.5 = (bf16[768,512]{1,0:T(8,128)(2,1)}, bf16[768,512]{1,0:T(8,128)(2,1)}, u32[]{:S(2)}, u32[]{:S(2)}) collective-permute-start(bf16[768,512]{1,0:T(8,128)(2,1)} %get-tuple-element.55), channel_id=1, source_target_pairs={{0,1},{4,5},{8,9},{12,13},{16,17},{20,21},{24,25},{28,29}} | collective-permute-start | bytes 2359304 | tf_op jit(solution)/shard_map/ppermute | solution.py:423
  46.0 23.1 %collective-permute-start.6 = (bf16[768,512]{1,0:T(8,128)(2,1)}, bf16[768,512]{1,0:T(8,128)(2,1)}, u32[]{:S(2)}, u32[]{:S(2)}) collective-permute-start(bf16[768,512]{1,0:T(8,128)(2,1)} %get-tuple-element.56), channel_id=1, source_target_pairs={{3,2},{7,6},{11,10},{15,14},{19,18},{23,22},{27,26},{31,30}} | collective-permute-start | bytes 2359304 | tf_op jit(solution)/shard_map/ppermute | solution.py:424
  54.5 10.9 %collective-permute-start.11 = (bf16[384,512]{1,0:T(8,128)(2,1)}, bf16[384,512]{1,0:T(8,128)(2,1)S(1)}, u32[]{:S(2)}, u32[]{:S(2)}) collective-permute-start(bf16[384,512]{1,0:T(8,128)(2,1)} %shard_map.85.refs_5_), channel_id=1, source_target_pairs={{0,8},{4,12},{8,0},{12,4},{1,9},{5,13},{9,1},{13,5},{2,10},{6,14},... | collective-permute-start | bytes 1179656 | tf_op jit(solution)/shard_map/ppermute | solution.py:467
  55.0 25.6 %collective-permute-start.13 = (bf16[512,1024]{1,0:T(8,128)(2,1)S(1)}, bf16[512,1024]{1,0:T(8,128)(2,1)S(1)}, u32[]{:S(2)}, u32[]{:S(2)}) collective-permute-start(bf16[512,1024]{1,0:T(8,128)(2,1)S(1)} %copy-done.1), channel_id=1, source_target_pairs={{0,16},{16,0},{1,17},{17,1},{2,18},{18,2},{3,19},{19,3},{4,20},{20... | collective-permute-start | bytes 3145736 | tf_op jit(solution)/shard_map/ppermute | solution.py:412
  55.7 13.5 %collective-permute-start.7 = (bf16[384,512]{1,0:T(8,128)(2,1)}, bf16[384,512]{1,0:T(8,128)(2,1)S(1)}, u32[]{:S(2)}, u32[]{:S(2)}) collective-permute-start(bf16[384,512]{1,0:T(8,128)(2,1)} %get-tuple-element.58.refs_1_), channel_id=1, source_target_pairs={{0,4},{4,0},{8,12},{12,8},{1,5},{5,1},{9,13},{13,9},{2,6},{6,2},{1... | collective-permute-start | bytes 1179656 | tf_op jit(solution)/shard_map/ppermute | solution.py:434
  65.4 64.7 %copy-start.8 = (bf16[384,512]{1,0:T(8,128)(2,1)}, bf16[384,512]{1,0:T(8,128)(2,1)S(1)}, u32[]{:S(2)}) copy-start(bf16[384,512]{1,0:T(8,128)(2,1)S(1)} %collective-permute-done.11.refs_7_) | copy-start | bytes 1179652
  65.4 3.7 %collective-permute-start.10 = (bf16[384,512]{1,0:T(8,128)(2,1)}, bf16[384,512]{1,0:T(8,128)(2,1)S(1)}, u32[]{:S(2)}, u32[]{:S(2)}) collective-permute-start(bf16[384,512]{1,0:T(8,128)(2,1)} %shard_map.85.refs_5_), channel_id=1, source_target_pairs={{0,4},{4,0},{8,12},{12,8},{1,5},{5,1},{9,13},{13,9},{2,6},{6,2},{1... | collective-permute-start | bytes 1179656 | tf_op jit(solution)/shard_map/ppermute | solution.py:434
  65.4 3.8 %collective-permute-start.9 = (bf16[384,512]{1,0:T(8,128)(2,1)}, bf16[384,512]{1,0:T(8,128)(2,1)S(1)}, u32[]{:S(2)}, u32[]{:S(2)}) collective-permute-start(bf16[384,512]{1,0:T(8,128)(2,1)} %collective-permute-done.8.refs_3_), channel_id=1, source_target_pairs={{0,4},{4,0},{8,12},{12,8},{1,5},{5,1},{9,13},{13,9},{2,6},{6,2},{1... | collective-permute-start | bytes 1179656 | tf_op jit(solution)/shard_map/ppermute | solution.py:435
  69.1 1.7 %collective-permute-start.12 = (bf16[384,512]{1,0:T(8,128)(2,1)S(1)}, bf16[384,512]{1,0:T(8,128)(2,1)S(1)}, u32[]{:S(2)}, u32[]{:S(2)}) collective-permute-start(bf16[384,512]{1,0:T(8,128)(2,1)S(1)} %collective-permute-done.11.refs_7_), channel_id=1, source_target_pairs={{0,4},{4,0},{8,12},{12,8},{1,5},{5,1},{9,13},{13,9},{2,6},{6,2},{1... | collective-permute-start | bytes 1179656 | tf_op jit(solution)/shard_map/ppermute | solution.py:435
  69.1 60.9 %copy-start.10 = (bf16[384,512]{1,0:T(8,128)(2,1)}, bf16[384,512]{1,0:T(8,128)(2,1)S(1)}, u32[]{:S(2)}) copy-start(bf16[384,512]{1,0:T(8,128)(2,1)S(1)} %collective-permute-done.7.refs_2_) | copy-start | bytes 1179652
  69.2 60.9 %copy-start.12 = (bf16[384,512]{1,0:T(8,128)(2,1)}, bf16[384,512]{1,0:T(8,128)(2,1)S(1)}, u32[]{:S(2)}) copy-start(bf16[384,512]{1,0:T(8,128)(2,1)S(1)} %collective-permute-done.10.refs_6_) | copy-start | bytes 1179652
  69.2 60.9 %copy-start.14 = (bf16[384,512]{1,0:T(8,128)(2,1)}, bf16[384,512]{1,0:T(8,128)(2,1)S(1)}, u32[]{:S(2)}) copy-start(bf16[384,512]{1,0:T(8,128)(2,1)S(1)} %collective-permute-done.9.refs_4_) | copy-start | bytes 1179652
  71.9 58.2 %copy-start.16 = (bf16[384,512]{1,0:T(8,128)(2,1)}, bf16[384,512]{1,0:T(8,128)(2,1)S(1)}, u32[]{:S(2)}) copy-start(bf16[384,512]{1,0:T(8,128)(2,1)S(1)} %collective-permute-done.12.refs_8_) | copy-start | bytes 1179652
  73.4 17.7 %collective-permute-start.14 = (bf16[768,512]{1,0:T(8,128)(2,1)S(1)}, bf16[768,512]{1,0:T(8,128)(2,1)S(1)}, u32[]{:S(2)}, u32[]{:S(2)}) collective-permute-start(bf16[768,512]{1,0:T(8,128)(2,1)S(1)} %get-tuple-element.62), channel_id=1, source_target_pairs={{0,1},{4,5},{8,9},{12,13},{16,17},{20,21},{24,25},{28,29}} | collective-permute-start | bytes 2359304 | tf_op jit(solution)/shard_map/ppermute | solution.py:423
  74.1 22.3 %collective-permute-start.15 = (bf16[768,512]{1,0:T(8,128)(2,1)S(1)}, bf16[768,512]{1,0:T(8,128)(2,1)S(1)}, u32[]{:S(2)}, u32[]{:S(2)}) collective-permute-start(bf16[768,512]{1,0:T(8,128)(2,1)S(1)} %get-tuple-element.63), channel_id=1, source_target_pairs={{3,2},{7,6},{11,10},{15,14},{19,18},{23,22},{27,26},{31,30}} | collective-permute-start | bytes 2359304 | tf_op jit(solution)/shard_map/ppermute | solution.py:424
  75.4 30.3 %collective-permute-start.16 = (bf16[512,1024]{1,0:T(8,128)(2,1)S(1)}, bf16[512,1024]{1,0:T(8,128)(2,1)S(1)}, u32[]{:S(2)}, u32[]{:S(2)}) collective-permute-start(bf16[512,1024]{1,0:T(8,128)(2,1)S(1)} %copy-done.2), channel_id=1, source_target_pairs={{0,16},{16,0},{1,17},{17,1},{2,18},{18,2},{3,19},{19,3},{4,20},{20... | collective-permute-start | bytes 3145736 | tf_op jit(solution)/shard_map/ppermute | solution.py:412
  85.1 21.3 %collective-permute-start.17 = (bf16[768,512]{1,0:T(8,128)(2,1)S(1)}, bf16[768,512]{1,0:T(8,128)(2,1)S(1)}, u32[]{:S(2)}, u32[]{:S(2)}) collective-permute-start(bf16[768,512]{1,0:T(8,128)(2,1)S(1)} %get-tuple-element.66), channel_id=1, source_target_pairs={{0,1},{1,2},{4,5},{5,6},{8,9},{9,10},{12,13},{13,14},{16,17},{17,1... | collective-permute-start | bytes 2359304 | tf_op jit(solution)/shard_map/ppermute | solution.py:423
  86.4 26.8 %collective-permute-start.18 = (bf16[768,512]{1,0:T(8,128)(2,1)S(1)}, bf16[768,512]{1,0:T(8,128)(2,1)S(1)}, u32[]{:S(2)}, u32[]{:S(2)}) collective-permute-start(bf16[768,512]{1,0:T(8,128)(2,1)S(1)} %get-tuple-element.67), channel_id=1, source_target_pairs={{2,1},{3,2},{6,5},{7,6},{10,9},{11,10},{14,13},{15,14},{18,17},{19... | collective-permute-start | bytes 2359304 | tf_op jit(solution)/shard_map/ppermute | solution.py:424
  99.8 25.7 %collective-permute-start.19 = (bf16[768,512]{1,0:T(8,128)(2,1)S(1)}, bf16[768,512]{1,0:T(8,128)(2,1)S(1)}, u32[]{:S(2)}, u32[]{:S(2)}) collective-permute-start(bf16[768,512]{1,0:T(8,128)(2,1)S(1)} %get-tuple-element.69), channel_id=1, source_target_pairs={{0,1},{1,2},{4,5},{5,6},{8,9},{9,10},{12,13},{13,14},{16,17},{17,1... | collective-permute-start | bytes 2359304 | tf_op jit(solution)/shard_map/ppermute | solution.py:423
  101.1 29.0 %collective-permute-start.20 = (bf16[768,512]{1,0:T(8,128)(2,1)S(1)}, bf16[768,512]{1,0:T(8,128)(2,1)S(1)}, u32[]{:S(2)}, u32[]{:S(2)}) collective-permute-start(bf16[768,512]{1,0:T(8,128)(2,1)S(1)} %get-tuple-element.70), channel_id=1, source_target_pairs={{2,1},{3,2},{6,5},{7,6},{10,9},{11,10},{14,13},{15,14},{18,17},{19... | collective-permute-start | bytes 2359304 | tf_op jit(solution)/shard_map/ppermute | solution.py:424
  105.7 39.1 %collective-permute-start.21 = (bf16[512,1024]{1,0:T(8,128)(2,1)S(1)}, bf16[512,1024]{1,0:T(8,128)(2,1)S(1)}, u32[]{:S(2)}, u32[]{:S(2)}) collective-permute-start(bf16[512,1024]{1,0:T(8,128)(2,1)S(1)} %copy-done.22), channel_id=1, source_target_pairs={{0,16},{16,0},{1,17},{17,1},{2,18},{18,2},{3,19},{19,3},{4,20},{20... | collective-permute-start | bytes 3145736 | tf_op jit(solution)/shard_map/ppermute | solution.py:412
  119.6 25.2 %collective-permute-start.22 = (bf16[768,512]{1,0:T(8,128)(2,1)S(1)}, bf16[768,512]{1,0:T(8,128)(2,1)S(1)}, u32[]{:S(2)}, u32[]{:S(2)}) collective-permute-start(bf16[768,512]{1,0:T(8,128)(2,1)S(1)} %get-tuple-element.73), channel_id=1, source_target_pairs={{0,1},{1,2},{2,3},{4,5},{5,6},{6,7},{8,9},{9,10},{10,11},{12,13},{... | collective-permute-start | bytes 2359304 | tf_op jit(solution)/shard_map/ppermute | solution.py:423
  121.5 25.4 %collective-permute-start.23 = (bf16[768,512]{1,0:T(8,128)(2,1)S(1)}, bf16[768,512]{1,0:T(8,128)(2,1)S(1)}, u32[]{:S(2)}, u32[]{:S(2)}) collective-permute-start(bf16[768,512]{1,0:T(8,128)(2,1)S(1)} %get-tuple-element.74), channel_id=1, source_target_pairs={{1,0},{2,1},{3,2},{5,4},{6,5},{7,6},{9,8},{10,9},{11,10},{13,12},{... | collective-permute-start | bytes 2359304 | tf_op jit(solution)/shard_map/ppermute | solution.py:424
  137.0 24.7 %collective-permute-start.24 = (bf16[768,512]{1,0:T(8,128)(2,1)}, bf16[768,512]{1,0:T(8,128)(2,1)S(1)}, u32[]{:S(2)}, u32[]{:S(2)}) collective-permute-start(bf16[768,512]{1,0:T(8,128)(2,1)} %get-tuple-element.76), channel_id=1, source_target_pairs={{0,1},{1,2},{2,3},{4,5},{5,6},{6,7},{8,9},{9,10},{10,11},{12,13},{... | collective-permute-start | bytes 2359304 | tf_op jit(solution)/shard_map/ppermute | solution.py:423
  138.9 24.1 %collective-permute-start.25 = (bf16[768,512]{1,0:T(8,128)(2,1)}, bf16[768,512]{1,0:T(8,128)(2,1)}, u32[]{:S(2)}, u32[]{:S(2)}) collective-permute-start(bf16[768,512]{1,0:T(8,128)(2,1)} %get-tuple-element.77), channel_id=1, source_target_pairs={{1,0},{2,1},{3,2},{5,4},{6,5},{7,6},{9,8},{10,9},{11,10},{13,12},{... | collective-permute-start | bytes 2359304 | tf_op jit(solution)/shard_map/ppermute | solution.py:424
  (23 other events, 216.0 us)
